TPU v7x, 32 devices: a whole 2x2x4 slice. The times are simulated.
32 devices in a mesh: seq: 8 (over z, x), head: 4 (over y, core).
Axes of the slice: x: 2, y: 2, z: 4, core: 2. Of those that a mesh axis runs over, the one named last changes fastest.
Arguments:
- att_query: bfloat16 [2048, 8, 128], P('seq', 'head'), may hold values from -9 to 9
- att_key: bfloat16 [2048, 8, 128], P('seq', 'head'), may hold values from -9 to 9
- att_value: bfloat16 [2048, 8, 128], P('seq', 'head'), may hold values from -6 to 6
- norm_gain: float32 [8, 128], P('head'), may hold values from 0.1 to 1.9
- dn_query: bfloat16 [2048, 8, 128], P('seq', 'head'), may hold values from -6 to 6
- dn_key: bfloat16 [2048, 8, 128], P('seq', 'head'), may hold values from -4 to 4
- write_rate: float32 [2048, 8], P('seq', 'head'), may hold values from 0.04 to 0.9
- log_decay: float32 [2048, 8], P('seq', 'head'), may hold values from -1 to 0
- out_grad: bfloat16 [2048, 8, 128], P('seq', 'head'), may hold values from -6 to 6
Outputs:
- block_out: bfloat16 [2048, 8, 128], P('seq', 'head')
- att_query_grad: bfloat16 [2048, 8, 128], P('seq', 'head')
- att_key_grad: bfloat16 [2048, 8, 128], P('seq', 'head')
- att_value_grad: bfloat16 [2048, 8, 128], P('seq', 'head')
- gain_grad: float32 [8, 128], P('head')
- dn_query_grad: bfloat16 [2048, 8, 128], P('seq', 'head')
- dn_key_grad: bfloat16 [2048, 8, 128], P('seq', 'head')
- rate_grad: float32 [2048, 8], P('seq', 'head')
- decay_grad: float32 [2048, 8], P('seq', 'head')
All inputs are finite; a program needn't handle non-finite values.
Results may differ from a plain program's by a relative error of at most 0.018.
Values may be sent and summed in bfloat16 or wider, within the bound.
A program may use at most 64 MiB of HBM per device.

v0:
```python
import jax
import jax.numpy as jnp
from jax import lax
from jax.sharding import PartitionSpec as P

WIN = 1024
CH = 64


MATMUL_ACCURACY = lax.Precision.HIGHEST
EPSILON = 1e-06


def shifted_2(block, axis, distance):
    devices = range(lax.axis_size(axis))
    route = [(i - distance, i) for i in devices if i - distance in devices]
    return lax.ppermute(block, axis, route)


def unit_rows(matrix):
    return matrix * lax.rsqrt(jnp.sum(matrix * matrix, axis=-1, keepdims=True) + EPSILON)


def delta_block(memory_state, pieces):
    query_vectors, key_vectors, value_rows, rate_rows, decay_rows = pieces
    length = key_vectors.shape[1]
    lower = jnp.tril(jnp.ones((length, length), jnp.float32))
    strict = lower - jnp.eye(length, dtype=jnp.float32)
    running_state = jnp.cumsum(decay_rows, axis=1)
    ratio = jnp.exp((running_state[:, :, None] - running_state[:, None, :]) * lower) * lower
    state_increment = jnp.exp(running_state)
    intersection = jnp.einsum("htk,hsk->hts", key_vectors, key_vectors, precision=MATMUL_ACCURACY)
    system = (
        jnp.eye(length, dtype=jnp.float32) + rate_rows[:, :, None] * ratio * strict * intersection
    )
    retrieved_values = jnp.einsum(
        "nex,nxp->nep", key_vectors, memory_state, precision=MATMUL_ACCURACY
    )
    target = rate_rows[:, :, None] * (value_rows - state_increment[:, :, None] * retrieved_values)
    newest_state = jax.scipy.linalg.solve_triangular(system, target, lower=True, unit_diagonal=True)
    local_scores = (
        jnp.einsum("htk,hsk->hts", query_vectors, key_vectors, precision=MATMUL_ACCURACY) * ratio
    )
    state_output = state_increment[:, :, None] * jnp.einsum(
        "nex,nxp->nep", query_vectors, memory_state, precision=MATMUL_ACCURACY
    )
    state_output = state_output + jnp.einsum(
        "hts,hsv->htv", local_scores, newest_state, precision=MATMUL_ACCURACY
    )
    retained_state = jnp.exp(running_state[:, -1:] - running_state)
    memory_state = jnp.exp(running_state[:, -1])[:, None, None] * memory_state + jnp.einsum(
        "wpa,wpn->wan",
        key_vectors * retained_state[:, :, None],
        newest_state,
        precision=MATMUL_ACCURACY,
    )
    return (memory_state, state_output)


def delta_sweep(memory_state, query_vectors, key_vectors, value_rows, rate_rows, decay_rows):
    head_count, length = (key_vectors.shape[0], key_vectors.shape[1])
    blocks = length // CH

    def cut_blocks(array):
        return jnp.moveaxis(array.reshape((head_count, blocks, CH) + array.shape[2:]), 1, 0)

    last_state, state_output = lax.scan(
        delta_block,
        memory_state,
        (
            cut_blocks(query_vectors),
            cut_blocks(key_vectors),
            cut_blocks(value_rows),
            cut_blocks(rate_rows),
            cut_blocks(decay_rows),
        ),
    )
    return (
        last_state,
        jnp.moveaxis(state_output, 0, 1).reshape(head_count, length, state_output.shape[-1]),
    )


def window_softmax(rows_here, keys_here, values_here, alive_keys):
    block_rows = rows_here.shape[0]
    span_rows = keys_here.shape[0]
    reach_back = span_rows - block_rows
    scores = jnp.einsum("qhd,khd->hqk", rows_here, keys_here) * rows_here.shape[-1] ** (-0.5)
    query_pos = jnp.arange(block_rows, dtype=jnp.int32)[:, None]
    key_pos = jnp.arange(span_rows, dtype=jnp.int32)[None, :]
    allowed = (key_pos > query_pos) & (key_pos <= query_pos + reach_back) & alive_keys[None, :]
    scores = jnp.where(allowed[None], scores, -1e30)
    shifted = jnp.exp(scores - jnp.max(scores, axis=-1, keepdims=True))
    weights_bf = (shifted / jnp.sum(shifted, axis=-1, keepdims=True)).astype(jnp.bfloat16)
    return jnp.einsum("hqk,khd->qhd", weights_bf.astype(jnp.float32), values_here)


def attend(query_vectors, key_vectors, value_rows, alive_keys):
    outputs = [window_softmax(query_vectors, key_vectors, value_rows, alive_keys)]
    return jnp.concatenate(outputs, axis=0)


def apply_map(matrix, operand):
    return jnp.einsum("hij,hjv->hiv", matrix, operand, precision=MATMUL_ACCURACY)


def body(
    att_query, att_key, att_value, norm_gain, dn_query, dn_key, write_rate, log_decay, out_grad
):
    row_count, head_count, head_width = att_query.shape
    rim_rows = min(WIN, row_count)
    reach_back = max(1, WIN // row_count)
    my_shard = lax.axis_index("seq")
    shard_count = lax.axis_size("seq")
    older_keys = []
    older_values = []
    for offset in range(reach_back):
        came_key, came_value = shifted_2((att_key, att_value), "seq", offset + 1)
        older_keys.insert(0, came_key)
        older_values.insert(0, came_value)
    all_keys = jnp.concatenate(older_keys + [att_key], axis=0).astype(jnp.float32)
    all_values = jnp.concatenate(older_values + [att_value], axis=0).astype(jnp.float32)
    alive_keys = my_shard * row_count - WIN + jnp.arange(WIN + row_count, dtype=jnp.int32) >= 0

    def attention_core(query_vectors, key_vectors, value_rows):
        return attend(query_vectors, key_vectors, value_rows, alive_keys)

    attended, attention_pull = jax.vjp(
        attention_core, att_query.astype(jnp.float32), all_keys, all_values
    )
    square_part = jnp.sum(attended * attended, axis=(1, 2))
    square_all = lax.psum(square_part, "head")
    features = head_count * lax.axis_size("head") * head_width
    inverse = lax.rsqrt(square_all / features + EPSILON)
    scaled = attended * inverse[:, None, None]
    values = (scaled * norm_gain[None]).astype(jnp.bfloat16)
    query_heads = jnp.swapaxes(dn_query, 0, 1).astype(jnp.float32)
    key_heads = jnp.swapaxes(dn_key, 0, 1).astype(jnp.float32)
    value_heads = jnp.swapaxes(values, 0, 1)
    rate_heads = write_rate.T
    decay_heads = log_decay.T
    identity = jnp.broadcast_to(
        jnp.eye(head_width, dtype=jnp.float32), (head_count, head_width, head_width)
    )
    seed_state = jnp.concatenate(
        [identity, jnp.zeros((head_count, head_width, head_width), jnp.float32)], axis=-1
    )
    folded_values = jnp.concatenate(
        [jnp.zeros(value_heads.shape, jnp.float32), value_heads.astype(jnp.float32)], axis=-1
    )
    summary, unused_out = delta_sweep(
        seed_state,
        unit_rows(query_heads),
        unit_rows(key_heads),
        folded_values,
        rate_heads,
        decay_heads,
    )
    carry_map = summary[..., :head_width]
    carry_add = summary[..., head_width:]
    empty_state = jnp.zeros_like(carry_add)

    def relay(turn, current):
        return shifted_2(apply_map(carry_map, current) + carry_add, "seq", 1)

    start_state = lax.fori_loop(0, shard_count - 1, relay, empty_state)

    def local_delta(start_in, query_in, key_in, value_in, rate_in, decay_in):
        last_state, state_output = delta_sweep(
            start_in,
            unit_rows(query_in),
            unit_rows(key_in),
            value_in.astype(jnp.float32),
            rate_in,
            decay_in,
        )
        return (state_output, last_state)

    (state_output, last_state), delta_pull = jax.vjp(
        local_delta, start_state, query_heads, key_heads, value_heads, rate_heads, decay_heads
    )
    cotangent = jnp.swapaxes(out_grad, 0, 1).astype(jnp.float32)
    own_back = delta_pull((cotangent, empty_state))[0]
    flipped = jnp.swapaxes(carry_map, 1, 2)

    def relay_back(turn, current):
        return shifted_2(apply_map(flipped, current) + own_back, "seq", -1)

    later_grad = lax.fori_loop(0, shard_count - 1, relay_back, empty_state)
    delta_grads = delta_pull((cotangent, later_grad))
    value_grad = jnp.swapaxes(delta_grads[3], 0, 1).astype(jnp.float32)
    weighted = value_grad * norm_gain[None]
    dot_part = jnp.sum(weighted * attended, axis=(1, 2))
    gain_part = jnp.sum(value_grad * scaled, axis=0)
    dot_all = lax.psum(dot_part, "head")
    gain_grad = lax.psum(gain_part, "seq")
    attended_grad = (
        inverse[:, None, None] * weighted
        - attended * (inverse * inverse * inverse * dot_all / features)[:, None, None]
    )
    query_grad, keys_grad, values_grad = attention_pull(attended_grad)
    own_key_grad = keys_grad[WIN:]
    own_value_grad = values_grad[WIN:]
    extra_key = jnp.zeros((rim_rows, head_count, head_width), jnp.float32)
    extra_value = jnp.zeros((rim_rows, head_count, head_width), jnp.float32)
    for offset in range(reach_back):
        segment = reach_back - 1 - offset
        sent_key = keys_grad[segment * rim_rows : (segment + 1) * rim_rows]
        sent_value = values_grad[segment * rim_rows : (segment + 1) * rim_rows]
        came_key, came_value = (
            shifted_2(sent_key.astype(jnp.bfloat16), "seq", -(offset + 1)).astype(sent_key.dtype),
            shifted_2(sent_value.astype(jnp.bfloat16), "seq", -(offset + 1)).astype(
                sent_value.dtype
            ),
        )
        extra_key = extra_key + came_key
        extra_value = extra_value + came_value
    own_key_grad = own_key_grad.at[row_count - rim_rows :].add(extra_key)
    own_value_grad = own_value_grad.at[row_count - rim_rows :].add(extra_value)
    block_out = jnp.swapaxes(state_output, 0, 1).astype(jnp.bfloat16)
    return (
        block_out,
        query_grad.astype(jnp.bfloat16),
        own_key_grad.astype(jnp.bfloat16),
        own_value_grad.astype(jnp.bfloat16),
        gain_grad,
        jnp.swapaxes(delta_grads[1], 0, 1).astype(jnp.bfloat16),
        jnp.swapaxes(delta_grads[2], 0, 1).astype(jnp.bfloat16),
        delta_grads[4].T,
        delta_grads[5].T,
    )


def solution(mesh):
    return jax.shard_map(
        body,
        mesh=mesh,
        in_specs=(
            P("seq", "head", None),
            P("seq", "head", None),
            P("seq", "head", None),
            P("head", None),
            P("seq", "head", None),
            P("seq", "head", None),
            P("seq", "head"),
            P("seq", "head"),
            P("seq", "head", None),
        ),
        out_specs=(
            P("seq", "head", None),
            P("seq", "head", None),
            P("seq", "head", None),
            P("seq", "head", None),
            P("head", None),
            P("seq", "head", None),
            P("seq", "head", None),
            P("seq", "head"),
            P("seq", "head"),
        ),
        check_vma=False,
    )
```

profile of v0, /device:TPU:10, one launch (start us, length us, event | category | flops | bytes accessed | tf_op | source)
XLA Modules:
  0.0 694.8 jit_solution(367765074566450671)
XLA Ops:
  54.8 69.7 %while.136 = (s32[]{:T(128)}, f32[2,128,256]{2,1,0:T(8,128)S(1)}, f32[4,2,64]{2,1,0:T(2,128)}, f32[4,2,64,128]{3,2,1,0:T(8,128)S(1)}, f32[4,2,64]{2,1,0:T(2,128)...) while((s32[]{:T(128)}, f32[2,128,256]{2,1,0:T(8,128)S(1)}, f32[4,2,64]{2,1,0:T(2,128)}, ...), condition=%wide.region_7.8_spmd, body=%wide.region_5.0_spmd.sunk | while | flops 138780736 | bytes 1925833 | solution.py:67
  58.7 11.2 %custom-call.55 = f32[2,1,64,64]{2,3,1,0:T(8,128)} custom-call(f32[2,1,64,64]{3,2,1,0:T(8,128)} %fusion.366), custom_call_target="InvertDiagBlocksLowerTriangular" | custom-call | tf_op jit(solution)/shard_map/while/body/eval_jaxpr/jit(_solve_triangular)/vmap()/triangular_solve | solution.py:40
  76.2 11.2 %custom-call.55 = f32[2,1,64,64]{2,3,1,0:T(8,128)} custom-call(f32[2,1,64,64]{3,2,1,0:T(8,128)} %fusion.366), custom_call_target="InvertDiagBlocksLowerTriangular" | custom-call | tf_op jit(solution)/shard_map/while/body/eval_jaxpr/jit(_solve_triangular)/vmap()/triangular_solve | solution.py:40
  93.5 11.2 %custom-call.55 = f32[2,1,64,64]{2,3,1,0:T(8,128)} custom-call(f32[2,1,64,64]{3,2,1,0:T(8,128)} %fusion.366), custom_call_target="InvertDiagBlocksLowerTriangular" | custom-call | tf_op jit(solution)/shard_map/while/body/eval_jaxpr/jit(_solve_triangular)/vmap()/triangular_solve | solution.py:40
  111.0 11.2 %custom-call.55 = f32[2,1,64,64]{2,3,1,0:T(8,128)} custom-call(f32[2,1,64,64]{3,2,1,0:T(8,128)} %fusion.366), custom_call_target="InvertDiagBlocksLowerTriangular" | custom-call | tf_op jit(solution)/shard_map/while/body/eval_jaxpr/jit(_solve_triangular)/vmap()/triangular_solve | solution.py:40
  128.3 62.9 %while.137 = (s32[]{:T(128)}, f32[2,128,128]{2,1,0:T(8,128)S(1)}, f32[2,128,128]{2,1,0:T(8,128)S(1)}, f32[2,128,128]{2,1,0:T(8,128)S(1)}, s32[]{:T(128)}) while((s32[]{:T(128)}, f32[2,128,128]{2,1,0:T(8,128)S(1)}, f32[2,128,128]{2,1,0:T(8,128)S(1)}, f32[2,128,128]{2,1,0:T(8,128)S(1)}, s32[]{:T(128)}) %tuple.298), condition=%wide.region_9.10_spmd, body=%wide.region_8.9_spmd.sunk | while | flops 50364416 | bytes 1048677 | solution.py:166
  194.9 105.8 %while.139 = (s32[]{:T(128)}, f32[2,128,128]{2,1,0:T(8,128)S(1)}, bf16[4,2,64,128]{3,2,1,0:T(8,128)(2,1)}, f32[4,2,64,64]{3,2,1,0:T(8,128)}, f32[4,2,64]{2,1,0:T...) while((s32[]{:T(128)}, f32[2,128,128]{2,1,0:T(8,128)S(1)}, ...), condition=%wide.region_13.14_spmd.clone.clone, body=%wide.region_11.13_spmd.clone.clone.sunk | while | flops 126304576 | bytes 3452789 | solution.py:67
  199.2 10.6 %custom-call.56 = f32[2,1,64,64]{2,3,1,0:T(8,128)S(1)} custom-call(f32[2,1,64,64]{3,2,1,0:T(8,128)} %get-tuple-element.3034), custom_call_target="InvertDiagBlocksLowerTriangular" | custom-call | tf_op jit(solution)/shard_map/jvp()/while/body/eval_jaxpr/jit(_solve_triangular)/vmap()/triangular_solve | solution.py:40
  225.7 10.6 %custom-call.56 = f32[2,1,64,64]{2,3,1,0:T(8,128)S(1)} custom-call(f32[2,1,64,64]{3,2,1,0:T(8,128)} %get-tuple-element.3034), custom_call_target="InvertDiagBlocksLowerTriangular" | custom-call | tf_op jit(solution)/shard_map/jvp()/while/body/eval_jaxpr/jit(_solve_triangular)/vmap()/triangular_solve | solution.py:40
  252.1 10.6 %custom-call.56 = f32[2,1,64,64]{2,3,1,0:T(8,128)S(1)} custom-call(f32[2,1,64,64]{3,2,1,0:T(8,128)} %get-tuple-element.3034), custom_call_target="InvertDiagBlocksLowerTriangular" | custom-call | tf_op jit(solution)/shard_map/jvp()/while/body/eval_jaxpr/jit(_solve_triangular)/vmap()/triangular_solve | solution.py:40
  278.6 10.6 %custom-call.56 = f32[2,1,64,64]{2,3,1,0:T(8,128)S(1)} custom-call(f32[2,1,64,64]{3,2,1,0:T(8,128)} %get-tuple-element.3034), custom_call_target="InvertDiagBlocksLowerTriangular" | custom-call | tf_op jit(solution)/shard_map/jvp()/while/body/eval_jaxpr/jit(_solve_triangular)/vmap()/triangular_solve | solution.py:40
  301.2 65.0 %while.141 = (s32[]{:T(128)}, f32[2,128,128]{2,1,0:T(8,128)S(1)}, f32[4,2,1,1]{1,3,2,0:T(1,128)}, f32[4,2,64,128]{3,2,1,0:T(8,128)}, f32[4,2,64,1]{2,1,3,0:T(2,1...) while((s32[]{:T(128)}, f32[2,128,128]{2,1,0:T(8,128)S(1)}, ...), condition=%wide.region_15.17_spmd.clone, body=%wide.region_14.16_spmd.clone.sunk | while | flops 100937792 | bytes 1587911 | solution.py:67
  305.0 9.8 %custom-call.59 = f32[2,1,64,64]{2,3,1,0:T(8,128)S(1)} custom-call(f32[2,1,64,64]{3,2,1,0:T(8,128)S(1)} %fusion.432), custom_call_target="InvertDiagBlocksLowerTriangular" | custom-call | tf_op jit(solution)/shard_map/transpose(jvp())/while/body/eval_jaxpr/jit(_solve_triangular)/vmap()/triangular_solve/custom-call.2 | solution.py:40
  321.3 9.8 %custom-call.59 = f32[2,1,64,64]{2,3,1,0:T(8,128)S(1)} custom-call(f32[2,1,64,64]{3,2,1,0:T(8,128)S(1)} %fusion.432), custom_call_target="InvertDiagBlocksLowerTriangular" | custom-call | tf_op jit(solution)/shard_map/transpose(jvp())/while/body/eval_jaxpr/jit(_solve_triangular)/vmap()/triangular_solve/custom-call.2 | solution.py:40
  337.5 9.8 %custom-call.59 = f32[2,1,64,64]{2,3,1,0:T(8,128)S(1)} custom-call(f32[2,1,64,64]{3,2,1,0:T(8,128)S(1)} %fusion.432), custom_call_target="InvertDiagBlocksLowerTriangular" | custom-call | tf_op jit(solution)/shard_map/transpose(jvp())/while/body/eval_jaxpr/jit(_solve_triangular)/vmap()/triangular_solve/custom-call.2 | solution.py:40
  353.8 9.8 %custom-call.59 = f32[2,1,64,64]{2,3,1,0:T(8,128)S(1)} custom-call(f32[2,1,64,64]{3,2,1,0:T(8,128)S(1)} %fusion.432), custom_call_target="InvertDiagBlocksLowerTriangular" | custom-call | tf_op jit(solution)/shard_map/transpose(jvp())/while/body/eval_jaxpr/jit(_solve_triangular)/vmap()/triangular_solve/custom-call.2 | solution.py:40
  366.2 57.5 %while.138 = (s32[]{:T(128)}, f32[2,128,128]{2,1,0:T(8,128)S(1)}, f32[2,128,128]{2,1,0:T(8,128)S(1)}, f32[2,128,128]{2,1,0:T(8,128)S(1)}, s32[]{:T(128)}) while((s32[]{:T(128)}, f32[2,128,128]{2,1,0:T(8,128)S(1)}, f32[2,128,128]{2,1,0:T(8,128)S(1)}, f32[2,128,128]{2,1,0:T(8,128)S(1)}, s32[]{:T(128)}) %tuple.319), condition=%wide.region_17.19_spmd, body=%wide.region_16.18_spmd.sunk | while | flops 50364416 | bytes 1048677 | solution.py:189
  368.5 6.2 collective-permute-done.1
  376.8 5.8 collective-permute-done.1
  384.9 5.8 collective-permute-done.1
  392.9 5.8 collective-permute-done.1
  400.9 6.7 collective-permute-done.1
  427.0 192.5 %while.140 = (s32[]{:T(128)}, f32[2,128,128]{2,1,0:T(8,128)S(1)}, f32[4,2,64,128]{3,2,1,0:T(8,128)}, f32[4,2,64,128]{3,2,1,0:T(8,128)}, bf16[4,2,64,128]{3,2,0,1...) while((s32[]{:T(128)}, f32[2,128,128]{2,1,0:T(8,128)S(1)}, ...), condition=%wide.region_29.31_spmd.clone.clone, body=%wide.region_18.30_spmd.clone.clone.sunk | while | flops 258761408 | bytes 5408265 | solution.py:67
  431.2 9.8 %custom-call.58 = f32[2,1,64,64]{2,3,1,0:T(8,128)S(1)} custom-call(f32[2,1,64,64]{3,2,1,0:T(8,128)S(1)} %add_bitcast_fusion.3), custom_call_target="InvertDiagBlocksLowerTriangular" | custom-call | tf_op jit(solution)/shard_map/transpose(jvp())/while/body/eval_jaxpr/jit(_solve_triangular)/vmap()/triangular_solve | solution.py:40
  445.5 9.8 %custom-call.57 = f32[2,1,64,64]{2,3,1,0:T(8,128)S(1)} custom-call(f32[2,1,64,64]{3,2,1,0:T(8,128)S(1)} %fusion.406), custom_call_target="InvertDiagBlocksLowerTriangular" | custom-call | tf_op jit(solution)/shard_map/transpose(jvp())/while/body/eval_jaxpr/jit(_solve_triangular)/vmap()/triangular_solve/custom-call.2 | solution.py:40
  479.3 9.8 %custom-call.58 = f32[2,1,64,64]{2,3,1,0:T(8,128)S(1)} custom-call(f32[2,1,64,64]{3,2,1,0:T(8,128)S(1)} %add_bitcast_fusion.3), custom_call_target="InvertDiagBlocksLowerTriangular" | custom-call | tf_op jit(solution)/shard_map/transpose(jvp())/while/body/eval_jaxpr/jit(_solve_triangular)/vmap()/triangular_solve | solution.py:40
  493.6 9.8 %custom-call.57 = f32[2,1,64,64]{2,3,1,0:T(8,128)S(1)} custom-call(f32[2,1,64,64]{3,2,1,0:T(8,128)S(1)} %fusion.406), custom_call_target="InvertDiagBlocksLowerTriangular" | custom-call | tf_op jit(solution)/shard_map/transpose(jvp())/while/body/eval_jaxpr/jit(_solve_triangular)/vmap()/triangular_solve/custom-call.2 | solution.py:40
  527.4 9.8 %custom-call.58 = f32[2,1,64,64]{2,3,1,0:T(8,128)S(1)} custom-call(f32[2,1,64,64]{3,2,1,0:T(8,128)S(1)} %add_bitcast_fusion.3), custom_call_target="InvertDiagBlocksLowerTriangular" | custom-call | tf_op jit(solution)/shard_map/transpose(jvp())/while/body/eval_jaxpr/jit(_solve_triangular)/vmap()/triangular_solve | solution.py:40
  541.6 9.8 %custom-call.57 = f32[2,1,64,64]{2,3,1,0:T(8,128)S(1)} custom-call(f32[2,1,64,64]{3,2,1,0:T(8,128)S(1)} %fusion.406), custom_call_target="InvertDiagBlocksLowerTriangular" | custom-call | tf_op jit(solution)/shard_map/transpose(jvp())/while/body/eval_jaxpr/jit(_solve_triangular)/vmap()/triangular_solve/custom-call.2 | solution.py:40
  575.5 9.8 %custom-call.58 = f32[2,1,64,64]{2,3,1,0:T(8,128)S(1)} custom-call(f32[2,1,64,64]{3,2,1,0:T(8,128)S(1)} %add_bitcast_fusion.3), custom_call_target="InvertDiagBlocksLowerTriangular" | custom-call | tf_op jit(solution)/shard_map/transpose(jvp())/while/body/eval_jaxpr/jit(_solve_triangular)/vmap()/triangular_solve | solution.py:40
  589.7 9.8 %custom-call.57 = f32[2,1,64,64]{2,3,1,0:T(8,128)S(1)} custom-call(f32[2,1,64,64]{3,2,1,0:T(8,128)S(1)} %fusion.406), custom_call_target="InvertDiagBlocksLowerTriangular" | custom-call | tf_op jit(solution)/shard_map/transpose(jvp())/while/body/eval_jaxpr/jit(_solve_triangular)/vmap()/triangular_solve/custom-call.2 | solution.py:40
  652.5 23.6 %psum.23 = f32[2,128]{1,0:T(2,128)} all-reduce(f32[2,128]{1,0:T(2,128)S(1)} %copy-done.42), channel_id=1, replica_groups=mesh['seq'=8,'head'=4] {'seq'}, use_global_device_ids=true, to_apply=%region_36.38 | all-reduce | flops 256 | bytes 2048 | tf_op jit(solution)/shard_map/psum | solution.py:196
  (625 shorter events, 432.5 us)
Async XLA Ops:
  1.7 24.4 %collective-permute-start.6 = (bf16[256,2,128]{2,0,1:T(8,128)(2,1)S(1)}, bf16[256,2,128]{2,0,1:T(8,128)(2,1)S(1)}, u32[]{:S(2)}, u32[]{:S(2)}) collective-permute-start(bf16[256,2,128]{2,0,1:T(8,128)(2,1)S(1)} %copy.247), channel_id=1, source_target_pairs={{0,16},{4,20},{8,24},{12,28},{1,17},{5,21},{9,25},{13,29},{2,18},{... | collective-permute-start | bytes 393224 | tf_op jit(solution)/shard_map/ppermute | solution.py:17
  6.2 21.8 %collective-permute-start.7 = (bf16[256,2,128]{2,0,1:T(8,128)(2,1)S(1)}, bf16[256,2,128]{2,0,1:T(8,128)(2,1)S(1)}, u32[]{:S(2)}, u32[]{:S(2)}) collective-permute-start(bf16[256,2,128]{2,0,1:T(8,128)(2,1)S(1)} %copy.247), channel_id=1, source_target_pairs={{0,12},{4,16},{8,20},{12,24},{16,28},{1,13},{5,17},{9,21},{13,25},... | collective-permute-start | bytes 393224 | tf_op jit(solution)/shard_map/ppermute | solution.py:17
  8.1 21.9 %collective-permute-start.8 = (bf16[256,2,128]{2,0,1:T(8,128)(2,1)S(1)}, bf16[256,2,128]{2,0,1:T(8,128)(2,1)S(1)}, u32[]{:S(2)}, u32[]{:S(2)}) collective-permute-start(bf16[256,2,128]{2,0,1:T(8,128)(2,1)S(1)} %copy.247), channel_id=1, source_target_pairs={{0,8},{4,12},{8,16},{12,20},{16,24},{20,28},{1,9},{5,13},{9,17},{1... | collective-permute-start | bytes 393224 | tf_op jit(solution)/shard_map/ppermute | solution.py:17
  10.0 21.9 %collective-permute-start.9 = (bf16[256,2,128]{2,0,1:T(8,128)(2,1)S(1)}, bf16[256,2,128]{2,0,1:T(8,128)(2,1)S(1)}, u32[]{:S(2)}, u32[]{:S(2)}) collective-permute-start(bf16[256,2,128]{2,0,1:T(8,128)(2,1)S(1)} %copy.247), channel_id=1, source_target_pairs={{0,4},{4,8},{8,12},{12,16},{16,20},{20,24},{24,28},{1,5},{5,9},{9,... | collective-permute-start | bytes 393224 | tf_op jit(solution)/shard_map/ppermute | solution.py:17
  24.8 10.7 %collective-permute-start.2 = (bf16[256,2,128]{0,2,1:T(8,128)(2,1)S(1)}, bf16[256,2,128]{0,2,1:T(8,128)(2,1)S(1)}, u32[]{:S(2)}, u32[]{:S(2)}) collective-permute-start(bf16[256,2,128]{0,2,1:T(8,128)(2,1)S(1)} %copy.242), channel_id=1, source_target_pairs={{0,16},{4,20},{8,24},{12,28},{1,17},{5,21},{9,25},{13,29},{2,18},{... | collective-permute-start | bytes 393224 | tf_op jit(solution)/shard_map/ppermute | solution.py:17
  26.1 12.2 %collective-permute-start.3 = (bf16[256,2,128]{0,2,1:T(8,128)(2,1)S(1)}, bf16[256,2,128]{0,2,1:T(8,128)(2,1)S(1)}, u32[]{:S(2)}, u32[]{:S(2)}) collective-permute-start(bf16[256,2,128]{0,2,1:T(8,128)(2,1)S(1)} %copy.242), channel_id=1, source_target_pairs={{0,12},{4,16},{8,20},{12,24},{16,28},{1,13},{5,17},{9,21},{13,25},... | collective-permute-start | bytes 393224 | tf_op jit(solution)/shard_map/ppermute | solution.py:17
  28.1 13.0 %collective-permute-start.4 = (bf16[256,2,128]{0,2,1:T(8,128)(2,1)S(1)}, bf16[256,2,128]{0,2,1:T(8,128)(2,1)S(1)}, u32[]{:S(2)}, u32[]{:S(2)}) collective-permute-start(bf16[256,2,128]{0,2,1:T(8,128)(2,1)S(1)} %copy.242), channel_id=1, source_target_pairs={{0,8},{4,12},{8,16},{12,20},{16,24},{20,28},{1,9},{5,13},{9,17},{1... | collective-permute-start | bytes 393224 | tf_op jit(solution)/shard_map/ppermute | solution.py:17
  30.0 12.5 %collective-permute-start.5 = (bf16[256,2,128]{0,2,1:T(8,128)(2,1)S(1)}, bf16[256,2,128]{0,2,1:T(8,128)(2,1)S(1)}, u32[]{:S(2)}, u32[]{:S(2)}) collective-permute-start(bf16[256,2,128]{0,2,1:T(8,128)(2,1)S(1)} %copy.242), channel_id=1, source_target_pairs={{0,4},{4,8},{8,12},{12,16},{16,20},{20,24},{24,28},{1,5},{5,9},{9,... | collective-permute-start | bytes 393224 | tf_op jit(solution)/shard_map/ppermute | solution.py:17
  129.3 8.4 %collective-permute-start = (f32[2,128,128]{2,1,0:T(8,128)}, f32[2,128,128]{2,1,0:T(8,128)S(1)}, u32[]{:S(2)}, u32[]{:S(2)}) collective-permute-start(f32[2,128,128]{2,1,0:T(8,128)} %convolution_add_fusion.30), channel_id=1, source_target_pairs={{0,4},{4,8},{8,12},{12,16},{16,20},{20,24},{24,28},{1,5},{5,9},{9,... | collective-permute-start | bytes 393224 | tf_op jit(solution)/shard_map/while/body/eval_jaxpr/ppermute | solution.py:17
  138.6 8.0 %collective-permute-start = (f32[2,128,128]{2,1,0:T(8,128)}, f32[2,128,128]{2,1,0:T(8,128)S(1)}, u32[]{:S(2)}, u32[]{:S(2)}) collective-permute-start(f32[2,128,128]{2,1,0:T(8,128)} %convolution_add_fusion.30), channel_id=1, source_target_pairs={{0,4},{4,8},{8,12},{12,16},{16,20},{20,24},{24,28},{1,5},{5,9},{9,... | collective-permute-start | bytes 393224 | tf_op jit(solution)/shard_map/while/body/eval_jaxpr/ppermute | solution.py:17
  147.5 8.0 %collective-permute-start = (f32[2,128,128]{2,1,0:T(8,128)}, f32[2,128,128]{2,1,0:T(8,128)S(1)}, u32[]{:S(2)}, u32[]{:S(2)}) collective-permute-start(f32[2,128,128]{2,1,0:T(8,128)} %convolution_add_fusion.30), channel_id=1, source_target_pairs={{0,4},{4,8},{8,12},{12,16},{16,20},{20,24},{24,28},{1,5},{5,9},{9,... | collective-permute-start | bytes 393224 | tf_op jit(solution)/shard_map/while/body/eval_jaxpr/ppermute | solution.py:17
  156.4 8.0 %collective-permute-start = (f32[2,128,128]{2,1,0:T(8,128)}, f32[2,128,128]{2,1,0:T(8,128)S(1)}, u32[]{:S(2)}, u32[]{:S(2)}) collective-permute-start(f32[2,128,128]{2,1,0:T(8,128)} %convolution_add_fusion.30), channel_id=1, source_target_pairs={{0,4},{4,8},{8,12},{12,16},{16,20},{20,24},{24,28},{1,5},{5,9},{9,... | collective-permute-start | bytes 393224 | tf_op jit(solution)/shard_map/while/body/eval_jaxpr/ppermute | solution.py:17
  165.3 8.0 %collective-permute-start = (f32[2,128,128]{2,1,0:T(8,128)}, f32[2,128,128]{2,1,0:T(8,128)S(1)}, u32[]{:S(2)}, u32[]{:S(2)}) collective-permute-start(f32[2,128,128]{2,1,0:T(8,128)} %convolution_add_fusion.30), channel_id=1, source_target_pairs={{0,4},{4,8},{8,12},{12,16},{16,20},{20,24},{24,28},{1,5},{5,9},{9,... | collective-permute-start | bytes 393224 | tf_op jit(solution)/shard_map/while/body/eval_jaxpr/ppermute | solution.py:17
  174.2 8.2 %collective-permute-start = (f32[2,128,128]{2,1,0:T(8,128)}, f32[2,128,128]{2,1,0:T(8,128)S(1)}, u32[]{:S(2)}, u32[]{:S(2)}) collective-permute-start(f32[2,128,128]{2,1,0:T(8,128)} %convolution_add_fusion.30), channel_id=1, source_target_pairs={{0,4},{4,8},{8,12},{12,16},{16,20},{20,24},{24,28},{1,5},{5,9},{9,... | collective-permute-start | bytes 393224 | tf_op jit(solution)/shard_map/while/body/eval_jaxpr/ppermute | solution.py:17
  183.2 8.0 %collective-permute-start = (f32[2,128,128]{2,1,0:T(8,128)}, f32[2,128,128]{2,1,0:T(8,128)S(1)}, u32[]{:S(2)}, u32[]{:S(2)}) collective-permute-start(f32[2,128,128]{2,1,0:T(8,128)} %convolution_add_fusion.30), channel_id=1, source_target_pairs={{0,4},{4,8},{8,12},{12,16},{16,20},{20,24},{24,28},{1,5},{5,9},{9,... | collective-permute-start | bytes 393224 | tf_op jit(solution)/shard_map/while/body/eval_jaxpr/ppermute | solution.py:17
  300.7 65.6 %copy-start.3 = (f32[2,128,128]{2,1,0:T(8,128)S(1)}, f32[2,128,128]{2,1,0:T(8,128)}, u32[]{:S(2)}) copy-start(f32[2,128,128]{2,1,0:T(8,128)} %get-tuple-element.3293) | copy-start | bytes 393220
  366.5 8.1 %collective-permute-start.1 = (f32[2,128,128]{2,1,0:T(8,128)S(1)}, f32[2,128,128]{2,1,0:T(8,128)S(1)}, u32[]{:S(2)}, u32[]{:S(2)}) collective-permute-start(f32[2,128,128]{2,1,0:T(8,128)S(1)} %convolution_add_fusion.31), channel_id=1, source_target_pairs={{4,0},{8,4},{12,8},{16,12},{20,16},{24,20},{28,24},{5,1},{9,5},{13... | collective-permute-start | bytes 393224 | tf_op jit(solution)/shard_map/while/body/eval_jaxpr/ppermute | solution.py:17
  374.9 7.8 %collective-permute-start.1 = (f32[2,128,128]{2,1,0:T(8,128)S(1)}, f32[2,128,128]{2,1,0:T(8,128)S(1)}, u32[]{:S(2)}, u32[]{:S(2)}) collective-permute-start(f32[2,128,128]{2,1,0:T(8,128)S(1)} %convolution_add_fusion.31), channel_id=1, source_target_pairs={{4,0},{8,4},{12,8},{16,12},{20,16},{24,20},{28,24},{5,1},{9,5},{13... | collective-permute-start | bytes 393224 | tf_op jit(solution)/shard_map/while/body/eval_jaxpr/ppermute | solution.py:17
  382.9 7.8 %collective-permute-start.1 = (f32[2,128,128]{2,1,0:T(8,128)S(1)}, f32[2,128,128]{2,1,0:T(8,128)S(1)}, u32[]{:S(2)}, u32[]{:S(2)}) collective-permute-start(f32[2,128,128]{2,1,0:T(8,128)S(1)} %convolution_add_fusion.31), channel_id=1, source_target_pairs={{4,0},{8,4},{12,8},{16,12},{20,16},{24,20},{28,24},{5,1},{9,5},{13... | collective-permute-start | bytes 393224 | tf_op jit(solution)/shard_map/while/body/eval_jaxpr/ppermute | solution.py:17
  391.0 7.8 %collective-permute-start.1 = (f32[2,128,128]{2,1,0:T(8,128)S(1)}, f32[2,128,128]{2,1,0:T(8,128)S(1)}, u32[]{:S(2)}, u32[]{:S(2)}) collective-permute-start(f32[2,128,128]{2,1,0:T(8,128)S(1)} %convolution_add_fusion.31), channel_id=1, source_target_pairs={{4,0},{8,4},{12,8},{16,12},{20,16},{24,20},{28,24},{5,1},{9,5},{13... | collective-permute-start | bytes 393224 | tf_op jit(solution)/shard_map/while/body/eval_jaxpr/ppermute | solution.py:17
  399.0 8.6 %collective-permute-start.1 = (f32[2,128,128]{2,1,0:T(8,128)S(1)}, f32[2,128,128]{2,1,0:T(8,128)S(1)}, u32[]{:S(2)}, u32[]{:S(2)}) collective-permute-start(f32[2,128,128]{2,1,0:T(8,128)S(1)} %convolution_add_fusion.31), channel_id=1, source_target_pairs={{4,0},{8,4},{12,8},{16,12},{20,16},{24,20},{28,24},{5,1},{9,5},{13... | collective-permute-start | bytes 393224 | tf_op jit(solution)/shard_map/while/body/eval_jaxpr/ppermute | solution.py:17
  407.9 7.8 %collective-permute-start.1 = (f32[2,128,128]{2,1,0:T(8,128)S(1)}, f32[2,128,128]{2,1,0:T(8,128)S(1)}, u32[]{:S(2)}, u32[]{:S(2)}) collective-permute-start(f32[2,128,128]{2,1,0:T(8,128)S(1)} %convolution_add_fusion.31), channel_id=1, source_target_pairs={{4,0},{8,4},{12,8},{16,12},{20,16},{24,20},{28,24},{5,1},{9,5},{13... | collective-permute-start | bytes 393224 | tf_op jit(solution)/shard_map/while/body/eval_jaxpr/ppermute | solution.py:17
  416.0 7.8 %collective-permute-start.1 = (f32[2,128,128]{2,1,0:T(8,128)S(1)}, f32[2,128,128]{2,1,0:T(8,128)S(1)}, u32[]{:S(2)}, u32[]{:S(2)}) collective-permute-start(f32[2,128,128]{2,1,0:T(8,128)S(1)} %convolution_add_fusion.31), channel_id=1, source_target_pairs={{4,0},{8,4},{12,8},{16,12},{20,16},{24,20},{28,24},{5,1},{9,5},{13... | collective-permute-start | bytes 393224 | tf_op jit(solution)/shard_map/while/body/eval_jaxpr/ppermute | solution.py:17
  640.1 38.1 %copy-start.10 = (f32[2,256]{0,1:T(8,128)S(1)}, f32[2,256]{0,1:T(8,128)}, u32[]{:S(2)}) copy-start(f32[2,256]{0,1:T(8,128)} %copy-done.9) | copy-start | bytes 6148
  642.6 37.0 %collective-permute-start.14 = (bf16[256,2,128]{0,2,1:T(8,128)(2,1)S(1)}, bf16[256,2,128]{0,2,1:T(8,128)(2,1)S(1)}, u32[]{:S(2)}, u32[]{:S(2)}) collective-permute-start(bf16[256,2,128]{0,2,1:T(8,128)(2,1)S(1)} %get-tuple-element.2469), channel_id=1, source_target_pairs={{4,0},{8,4},{12,8},{16,12},{20,16},{24,20},{28,24},{5,1},{9,5},{13... | collective-permute-start | bytes 393224 | tf_op jit(solution)/shard_map/ppermute | solution.py:17
  644.5 37.5 %collective-permute-start.15 = (bf16[256,2,128]{0,2,1:T(8,128)(2,1)S(1)}, bf16[256,2,128]{0,2,1:T(8,128)(2,1)S(1)}, u32[]{:S(2)}, u32[]{:S(2)}) collective-permute-start(bf16[256,2,128]{0,2,1:T(8,128)(2,1)S(1)} %get-tuple-element.2472), channel_id=1, source_target_pairs={{8,0},{12,4},{16,8},{20,12},{24,16},{28,20},{9,1},{13,5},{17,9},{2... | collective-permute-start | bytes 393224 | tf_op jit(solution)/shard_map/ppermute | solution.py:17
  646.5 37.5 %collective-permute-start.16 = (bf16[256,2,128]{0,2,1:T(8,128)(2,1)S(1)}, bf16[256,2,128]{0,2,1:T(8,128)(2,1)S(1)}, u32[]{:S(2)}, u32[]{:S(2)}) collective-permute-start(bf16[256,2,128]{0,2,1:T(8,128)(2,1)S(1)} %get-tuple-element.2471), channel_id=1, source_target_pairs={{12,0},{16,4},{20,8},{24,12},{28,16},{13,1},{17,5},{21,9},{25,13},... | collective-permute-start | bytes 393224 | tf_op jit(solution)/shard_map/ppermute | solution.py:17
  648.4 36.9 %collective-permute-start.17 = (bf16[256,2,128]{0,2,1:T(8,128)(2,1)S(1)}, bf16[256,2,128]{0,2,1:T(8,128)(2,1)S(1)}, u32[]{:S(2)}, u32[]{:S(2)}) collective-permute-start(bf16[256,2,128]{0,2,1:T(8,128)(2,1)S(1)} %get-tuple-element.2470), channel_id=1, source_target_pairs={{16,0},{20,4},{24,8},{28,12},{17,1},{21,5},{25,9},{29,13},{18,2},{... | collective-permute-start | bytes 393224 | tf_op jit(solution)/shard_map/ppermute | solution.py:17
  649.7 37.4 %collective-permute-start.10 = (bf16[256,2,128]{2,0,1:T(8,128)(2,1)S(1)}, bf16[256,2,128]{2,0,1:T(8,128)(2,1)S(1)}, u32[]{:S(2)}, u32[]{:S(2)}) collective-permute-start(bf16[256,2,128]{2,0,1:T(8,128)(2,1)S(1)} %get-tuple-element.2473), channel_id=1, source_target_pairs={{4,0},{8,4},{12,8},{16,12},{20,16},{24,20},{28,24},{5,1},{9,5},{13... | collective-permute-start | bytes 393224 | tf_op jit(solution)/shard_map/ppermute | solution.py:17
  679.6 8.2 %collective-permute-start.11 = (bf16[256,2,128]{2,0,1:T(8,128)(2,1)S(1)}, bf16[256,2,128]{2,0,1:T(8,128)(2,1)S(1)}, u32[]{:S(2)}, u32[]{:S(2)}) collective-permute-start(bf16[256,2,128]{2,0,1:T(8,128)(2,1)S(1)} %get-tuple-element.2476), channel_id=1, source_target_pairs={{8,0},{12,4},{16,8},{20,12},{24,16},{28,20},{9,1},{13,5},{17,9},{2... | collective-permute-start | bytes 393224 | tf_op jit(solution)/shard_map/ppermute | solution.py:17
  682.0 9.0 %collective-permute-start.12 = (bf16[256,2,128]{2,0,1:T(8,128)(2,1)S(1)}, bf16[256,2,128]{2,0,1:T(8,128)(2,1)S(1)}, u32[]{:S(2)}, u32[]{:S(2)}) collective-permute-start(bf16[256,2,128]{2,0,1:T(8,128)(2,1)S(1)} %get-tuple-element.2475), channel_id=1, source_target_pairs={{12,0},{16,4},{20,8},{24,12},{28,16},{13,1},{17,5},{21,9},{25,13},... | collective-permute-start | bytes 393224 | tf_op jit(solution)/shard_map/ppermute | solution.py:17
  684.0 9.0 %collective-permute-start.13 = (bf16[256,2,128]{2,0,1:T(8,128)(2,1)S(1)}, bf16[256,2,128]{2,0,1:T(8,128)(2,1)S(1)}, u32[]{:S(2)}, u32[]{:S(2)}) collective-permute-start(bf16[256,2,128]{2,0,1:T(8,128)(2,1)S(1)} %get-tuple-element.2474), channel_id=1, source_target_pairs={{16,0},{20,4},{24,8},{28,12},{17,1},{21,5},{25,9},{29,13},{18,2},{... | collective-permute-start | bytes 393224 | tf_op jit(solution)/shard_map/ppermute | solution.py:17
  (46 other events, 424.0 us)
where the time goes:
time: 709 us; the launch traced here: 695 us
  other arithmetic  272 us (38%)
  matrix products  159 us (22%)
  starting transfers between devices  82.4 us (12%)
  waiting for transfers between devices  76 us (11%)
  local copies, waits for them, and re-layouts  67.5 us (10%)
  blocking collectives  35 us (5%)
    another operation x72, other arithmetic, delta_block(): jax.scipy.linalg.solve_triangular(system, target, lower=True, unit_diagon...  217 us
    ppermute x30, starting transfers between devices, shifted_2(): return lax.ppermute(block, axis, route)  82.4 us
    ppermute x30, waiting for transfers between devices, shifted_2(): return lax.ppermute(block, axis, route)  76 us
    psum x1, blocking collectives, body(): gain_grad = lax.psum(gain_part, 'seq')  23.6 us
    dot_general x16, matrix products, delta_block(): jnp.einsum('nex,nxp->nep', query_vectors, memory_state, precision=MATMUL_...  22.6 us
    dot_general x20, matrix products, delta_block(): jnp.einsum('nex,nxp->nep', key_vectors, memory_state, precision=MATMUL_AC...  20.3 us
    another operation x20, matrix products, delta_block(): jax.scipy.linalg.solve_triangular(system, target, lower=True, unit_diagon...  19.7 us
    dot_general x16, matrix products, delta_block(): jnp.einsum('htk,hsk->hts', key_vectors, key_vectors, precision=MATMUL_ACC...  18.5 us
  transfers between devices with their start and end apart: 30, of which 21 were waited for; matrix products, arithmetic and copies ran while one was open for 3% of the time, Pallas kernels for 0%

commit v1 on v0

v1 whole, which is shorter than its diff:
```python
import functools

import jax
import jax.numpy as jnp
from jax import lax
from jax.experimental import pallas as pl
from jax.experimental.pallas import tpu as pltpu
from jax.sharding import PartitionSpec as P

WIN = 1024
EPSILON = 1e-06
MESH = pl.DeviceIdType.MESH
F32 = jnp.float32
BF = jnp.bfloat16
NN = (((1,), (0,)), ((), ()))
NT = (((1,), (1,)), ((), ()))
TN = (((0,), (0,)), ((), ()))


def dot(a, b, dims=NN):
    return lax.dot_general(a.astype(BF), b.astype(BF), dims, preferred_element_type=F32)


def halves(a):
    high = a.astype(BF)
    return high, (a - high.astype(F32)).astype(BF)


def dot3(a, b, dims=NN):
    if a.dtype == BF and b.dtype == BF:
        return dot(a, b, dims)
    if a.dtype == BF:
        bh, bl = halves(b)
        return dot(a, bh, dims) + dot(a, bl, dims)
    if b.dtype == BF:
        ah, al = halves(a)
        return dot(ah, b, dims) + dot(al, b, dims)
    ah, al = halves(a)
    bh, bl = halves(b)
    return dot(ah, bh, dims) + (dot(ah, bl, dims) + dot(al, bh, dims))


def row_sum(a):
    return jnp.sum(a, axis=1, keepdims=True)


def col_sum(a):
    return jnp.sum(a, axis=0, keepdims=True)


def kernel(
    seq_n, head_n, reach, rounds, heads, width,
    q_ref, k_ref, v_ref, gain_ref, dq_ref, dk_ref, rate_ref, decay_ref, og_ref,
    out_ref, qg_ref, kg_ref, vg_ref, gg_ref, dqg_ref, dkg_ref, rg_ref, cg_ref,
    kv_in, fm_out, fm_in, fa_out, fa_in, bk_out, bk_in, hs_out, hs_in, gn_out, gn_in, gr_out, gr_in,
    t_s, ratio_s, p_s, kkr_s, score_s, weight_s,
    kv_ss, kv_rs, fm_ss, fm_rs, fa_ss, fa_rs, bk_ss, bk_rs, hs_ss, hs_rs, gn_ss, gn_rs, gr_ss, gr_rs,
):
    rows = q_ref.shape[0]
    me = lax.axis_index("seq")
    my_head = lax.axis_index("head")
    cols = [slice(h * width, (h + 1) * width) for h in range(heads)]

    def seq_copy(src, dst, send_sem, recv_sem, shift):
        target = lax.rem(me + (shift + seq_n), seq_n)
        return pltpu.make_async_remote_copy(
            src_ref=src, dst_ref=dst, send_sem=send_sem, recv_sem=recv_sem,
            device_id={"seq": target}, device_id_type=MESH,
        )

    def head_copy(step):
        target = lax.rem(my_head + step, head_n)
        return pltpu.make_async_remote_copy(
            src_ref=hs_out, dst_ref=hs_in.at[step - 1], send_sem=hs_ss.at[step - 1],
            recv_sem=hs_rs.at[step - 1], device_id={"head": target}, device_id_type=MESH,
        )

    def kv_copies(b):
        return [
            seq_copy(ref, kv_in.at[b - 1, i], kv_ss.at[b - 1, i], kv_rs.at[b - 1, i], b)
            for i, ref in enumerate((k_ref, v_ref))
        ]

    def grad_copies(b):
        return [
            seq_copy(gr_out.at[b - 1, i], gr_in.at[b - 1, i], gr_ss.at[b - 1, i], gr_rs.at[b - 1, i], -b)
            for i in range(2)
        ]

    def fm_copy(r):
        return seq_copy(fm_out.at[r], fm_in.at[r], fm_ss.at[r], fm_rs.at[r], 1 << r)

    def fa_copy(r):
        return seq_copy(fa_out.at[r], fa_in.at[r], fa_ss.at[r], fa_rs.at[r], 1 << r)

    def bk_copy(r):
        return seq_copy(bk_out.at[r], bk_in.at[r], bk_ss.at[r], bk_rs.at[r], -(1 << r))

    def gain_copy(step):
        return seq_copy(gn_out, gn_in.at[step - 1], gn_ss.at[step - 1], gn_rs.at[step - 1], step)

    def up_ok(d):
        return me + d < seq_n

    def down_ok(d):
        return me - d >= 0

    def start_if(condition, copies):
        @pl.when(condition)
        def _():
            for copy in copies:
                copy.start()

    def recv_if(condition, copies):
        @pl.when(condition)
        def _():
            for copy in copies:
                copy.wait_recv()

    def send_wait_if(condition, copies):
        @pl.when(condition)
        def _():
            for copy in copies:
                copy.wait_send()

    for b in range(1, reach + 1):
        @pl.when(jnp.logical_not(down_ok(b)))
        def _():
            kv_in[b - 1] = jnp.zeros(kv_in.shape[1:], BF)

        @pl.when(jnp.logical_not(up_ok(b)))
        def _():
            gr_in[b - 1] = jnp.zeros(gr_in.shape[1:], BF)
    for r in range(rounds):
        @pl.when(jnp.logical_not(down_ok(1 << r)))
        def _():
            fm_in[r] = jnp.zeros(fm_in.shape[1:], BF)
            fa_in[r] = jnp.zeros(fa_in.shape[1:], BF)

        @pl.when(jnp.logical_not(up_ok(1 << r)))
        def _():
            bk_in[r] = jnp.zeros(bk_in.shape[1:], BF)

    barrier = pltpu.get_barrier_semaphore()
    for step in range(1, seq_n):
        pl.semaphore_signal(barrier, inc=1, device_id={"seq": lax.rem(me + step, seq_n)}, device_id_type=MESH)
    for step in range(1, head_n):
        pl.semaphore_signal(barrier, inc=1, device_id={"head": lax.rem(my_head + step, head_n)}, device_id_type=MESH)
    pl.semaphore_wait(barrier, seq_n + head_n - 2)

    for b in range(1, reach + 1):
        start_if(up_ok(b), kv_copies(b))

    at_row = lax.broadcasted_iota(jnp.int32, (rows, rows), 0)
    at_col = lax.broadcasted_iota(jnp.int32, (rows, rows), 1)
    lower = at_row >= at_col
    strict = at_row > at_col
    diagonal = at_row == at_col
    eye = diagonal.astype(F32)

    def to_row(column):
        return col_sum(jnp.where(diagonal, column, 0.0))

    def to_col(line):
        return row_sum(jnp.where(diagonal, line, 0.0))

    state = []
    for h in range(heads):
        xq, xk, dout = dq_ref[:, cols[h]], dk_ref[:, cols[h]], og_ref[:, cols[h]]
        fq, fk = xq.astype(F32), xk.astype(F32)
        rq = lax.rsqrt(row_sum(fq * fq) + EPSILON)
        rk = lax.rsqrt(row_sum(fk * fk) + EPSILON)
        rk_row = to_row(rk)
        rate = rate_ref[:, h : h + 1]
        decay_row = to_row(decay_ref[:, h : h + 1])
        cum = row_sum(jnp.where(lower, decay_row, 0.0))
        cum_row = to_row(cum)
        ratio = jnp.where(lower, jnp.exp(jnp.where(lower, cum - cum_row, 0.0)), 0.0)
        gamma = jnp.exp(cum)
        last = cum[rows - 1 : rows, :]
        retain = jnp.exp(last - cum)
        whole = jnp.exp(last)
        kkr = dot(xk, xk, NT) * (rk * rk_row) * ratio
        p = dot(xq, xk, NT) * (rq * rk_row) * ratio
        ratio_s[h] = ratio
        kkr_s[h] = kkr
        p_s[h] = p
        system = jnp.where(strict, rate * kkr, 0.0)
        state.append(dict(
            rq=rq, rk=rk, rate=rate, gamma=gamma, retain=retain, whole=whole,
            q=fq * rq, k=fk * rk, system=system, dout=dout,
        ))
    inverse_of = []
    for h in range(heads):
        off = ((at_row >> 1) == (at_col >> 1))
        inverse_of.append(eye - jnp.where(off, state[h]["system"], 0.0))
    level = 1
    while (1 << level) < rows:
        off = ((at_row >> (level + 1)) == (at_col >> (level + 1))) & ((at_row >> level) != (at_col >> level))
        for h in range(heads):
            x = inverse_of[h]
            y = dot3(x, jnp.where(off, state[h]["system"], 0.0))
            inverse_of[h] = x - dot3(y, x)
        level += 1
    for h in range(heads):
        s = state[h]
        t = inverse_of[h]
        t_s[h] = t
        kr = s["k"] * s["retain"]
        w = dot3(t, s["rate"] * s["gamma"] * s["k"])
        y = s["gamma"] * s["q"] - dot3(p_s[h], w)
        small = lax.broadcasted_iota(jnp.int32, (width, width), 0) == lax.broadcasted_iota(jnp.int32, (width, width), 1)
        diag = jnp.where(small, s["whole"], 0.0)
        s["kr"], s["w"] = kr, w
        s["fm"] = diag - dot3(kr, w, TN)
        s["bm"] = diag - dot3(w, kr, TN)
        s["bb"] = dot3(y, s["dout"], TN)
        s["em"] = s["ea"] = s["eb"] = s["ebm"] = None

    def block(h, part=0, parts=1):
        return slice((part * heads + h) * width, (part * heads + h + 1) * width)

    def forward_send(r):
        for h in range(heads):
            fm_out[r, block(h)] = state[h]["fm"].astype(BF)
        start_if(up_ok(1 << r), [fm_copy(r)])

    def back_send(r):
        for h in range(heads):
            bk_out[r, block(h)] = state[h]["bm"].astype(BF)
            bk_out[r, block(h, 1)] = state[h]["bb"].astype(BF)
        start_if(down_ok(1 << r), [bk_copy(r)])

    def back_take(r):
        recv_if(up_ok(1 << r), [bk_copy(r)])
        for h in range(heads):
            s = state[h]
            m, b = bk_in[r, block(h)], bk_in[r, block(h, 1)]
            if r == 0:
                s["ebm"], s["eb"] = m.astype(F32), b.astype(F32)
            else:
                s["eb"] = s["eb"] + dot(s["ebm"], b)
                if r < rounds - 1:
                    s["ebm"] = dot(s["ebm"], m)
            if r < rounds - 1:
                s["bb"] = s["bb"] + dot(s["bm"], b)
                s["bm"] = dot(s["bm"], m)

    def forward_take(r):
        recv_if(down_ok(1 << r), [fm_copy(r)])
        for h in range(heads):
            s = state[h]
            m = fm_in[r, block(h)]
            s.setdefault("own", []).append(s["fm"])
            if r == 0:
                s["before"] = [None, m.astype(F32)]
            else:
                s["before"].append(dot(s["before"][-1], m) if r < rounds - 1 else None)
            if r < rounds - 1:
                s["fm"] = dot(s["fm"], m)

    scale = width ** (-0.5)

    def score_block(b):
        if b > 0:
            recv_if(down_ok(b), kv_copies(b))
        for h in range(heads):
            keys = k_ref[:, cols[h]] if b == 0 else kv_in[b - 1, 0, :, cols[h]]
            sc = dot(q_ref[:, cols[h]], keys, NT) * scale
            if b == 0:
                sc = jnp.where(lower, sc, -1e30)
            elif b == reach:
                sc = jnp.where(jnp.logical_and(at_col > at_row, down_ok(b)), sc, -1e30)
            else:
                sc = jnp.where(down_ok(b), sc, -1e30)
            score_s[h, b] = sc

    back_send(0)
    forward_send(0)
    score_block(0)
    for r in range(rounds):
        back_take(r)
        if r < rounds - 1:
            back_send(r + 1)
        forward_take(r)
        if r < rounds - 1:
            forward_send(r + 1)
    for h in range(heads):
        s = state[h]
        dn = dot3(p_s[h], s["dout"], TN) + dot3(s["kr"], s["eb"])
        s["r"] = dot3(t_s[h], dn, TN)
        s["vg"] = (s["rate"] * s["r"]).astype(BF).astype(F32)
    for b in range(1, reach + 1):
        score_block(b)
    square = 0.0
    inner = 0.0
    for h in range(heads):
        s = state[h]
        top = row_sum(jnp.zeros((rows, 128), F32)) - 1e30
        for b in range(reach + 1):
            top = jnp.maximum(top, jnp.max(score_s[h, b], axis=1, keepdims=True))
        total = 0.0
        for b in range(reach + 1):
            e = jnp.exp(score_s[h, b] - top)
            score_s[h, b] = e
            total = total + row_sum(e)
        attended = 0.0
        for b in range(reach + 1):
            w = score_s[h, b] / total
            score_s[h, b] = w
            wb = w.astype(BF)
            weight_s[h, b] = wb
            values = v_ref[:, cols[h]] if b == 0 else kv_in[b - 1, 1, :, cols[h]]
            attended = attended + dot(wb, values)
        s["att"] = attended
        s["weighted"] = s["vg"] * gain_ref[h : h + 1, :]
        square = square + row_sum(attended * attended)
        inner = inner + row_sum(s["weighted"] * attended)
    hs_out[0:8] = jnp.broadcast_to(to_row(square), (8, rows))
    hs_out[8:16] = jnp.broadcast_to(to_row(inner), (8, rows))
    for step in range(1, head_n):
        head_copy(step).start()
    sums = hs_out[...]
    for step in range(1, head_n):
        head_copy(step).wait_recv()
        sums = sums + hs_in[step - 1]
    features = heads * head_n * width
    inverse = lax.rsqrt(to_col(sums[0:1]) / features + EPSILON)
    slope = inverse * inverse * inverse * to_col(sums[8:9]) / features
    gains = []
    for h in range(heads):
        s = state[h]
        scaled = s["att"] * inverse
        gains.append(col_sum(s["vg"] * scaled))
        s["val"] = (scaled * gain_ref[h : h + 1, :]).astype(BF)
        s["datt"] = (inverse * s["weighted"] - s["att"] * slope).astype(BF)
        s["u0"] = dot3(t_s[h], s["rate"] * s["val"].astype(F32))
        s["fa"] = dot3(s["kr"], s["u0"], TN)

    def add_send(r):
        for h in range(heads):
            fa_out[r, block(h)] = state[h]["fa"].astype(BF)
        start_if(up_ok(1 << r), [fa_copy(r)])

    def add_take(r):
        recv_if(down_ok(1 << r), [fa_copy(r)])
        for h in range(heads):
            s = state[h]
            a = fa_in[r, block(h)]
            s["ea"] = a.astype(F32) if r == 0 else s["ea"] + dot(s["before"][r], a)
            if r < rounds - 1:
                s["fa"] = s["fa"] + dot(s["own"][r], a)

    add_send(0)
    gn_out[...] = jnp.concatenate(gains + [jnp.zeros((8 - heads, width), F32)], axis=0)
    for step in range(1, seq_n):
        gain_copy(step).start()

    for h in range(heads):
        s = state[h]
        mean = 0.0
        for b in range(reach + 1):
            values = v_ref[:, cols[h]] if b == 0 else kv_in[b - 1, 1, :, cols[h]]
            dw = dot(s["datt"], values, NT).astype(BF).astype(F32)
            mean = mean + row_sum(dw * score_s[h, b])
        s["mean"] = mean
        s["dqa"] = 0.0
    own_grad = []
    for b in list(range(reach, 0, -1)) + [0]:
        for h in range(heads):
            s = state[h]
            keys = k_ref[:, cols[h]] if b == 0 else kv_in[b - 1, 0, :, cols[h]]
            values = v_ref[:, cols[h]] if b == 0 else kv_in[b - 1, 1, :, cols[h]]
            dw = dot(s["datt"], values, NT).astype(BF).astype(F32)
            ds = (score_s[h, b] * (dw - s["mean"]) * scale).astype(BF)
            s["dqa"] = s["dqa"] + dot(ds, keys)
            dkey = dot(ds, q_ref[:, cols[h]], TN)
            dval = dot(weight_s[h, b], s["datt"], TN)
            if b > 0:
                gr_out[b - 1, 0, :, cols[h]] = dkey.astype(BF)
                gr_out[b - 1, 1, :, cols[h]] = dval.astype(BF)
            else:
                own_grad.append((dkey, dval))
        if b > 0:
            start_if(down_ok(b), grad_copies(b))
        if reach - b < rounds and b > 0:
            r = reach - b
            add_take(r)
            if r < rounds - 1:
                add_send(r + 1)
    for r in range(reach, rounds):
        add_take(r)
        if r < rounds - 1:
            add_send(r + 1)
    for h in range(heads):
        qg_ref[:, cols[h]] = state[h]["dqa"].astype(BF)

    for h in range(heads):
        s = state[h]
        start, later = s["ea"], s["eb"]
        q, k, rate, gamma, retain = s["q"], s["k"], s["rate"], s["gamma"], s["retain"]
        r, dout = s["r"], s["dout"]
        fout = dout.astype(F32)
        ks = dot(k, start)
        qs = dot(q, start)
        new = s["u0"] - dot3(s["w"], start)
        p = p_s[h]
        out_ref[:, cols[h]] = (gamma * qs + dot(p, new)).astype(BF)
        dp = dot(dout, new, NT)
        da = jnp.where(strict, -dot(r, new, NT), 0.0)
        ratio, kkr = ratio_s[h], kkr_s[h]
        dqk = (dp * ratio)
        dkk = da * (rate * ratio)
        ak = da * kkr
        e = dp * p + ak * rate
        vals = s["val"].astype(F32)
        rate_grad = row_sum(ak) + row_sum(r * (vals - gamma * ks))
        down = -rate * r
        dgamma = row_sum(down * ks + fout * qs)
        dks = gamma * down
        dq = dot(gamma * fout, start, NT) + dot(dqk, k)
        dkr = dot(new, later, NT)
        dk = (
            dot(dks, start, NT) + dot(dqk, q, TN) + dot(dkk, k) + dot(dkk, k, TN) + retain * dkr
        )
        dret = row_sum(dkr * k) * retain
        dlast = col_sum(dret) + s["whole"] * col_sum(row_sum(later * start))
        dcum = to_row(row_sum(e) + dgamma * gamma - dret) - col_sum(e)
        cg_ref[:, h : h + 1] = row_sum(jnp.where(at_col >= at_row, dcum, 0.0)) + dlast
        rg_ref[:, h : h + 1] = rate_grad
        dqg_ref[:, cols[h]] = (s["rq"] * (dq - q * row_sum(q * dq))).astype(BF)
        dkg_ref[:, cols[h]] = (s["rk"] * (dk - k * row_sum(k * dk))).astype(BF)

    gain = gn_out[...]
    for step in range(1, seq_n):
        gain_copy(step).wait_recv()
        gain = gain + gn_in[step - 1]
    gg_ref[...] = gain[0:heads]
    for b in range(reach, 0, -1):
        recv_if(up_ok(b), grad_copies(b))
    for h in range(heads):
        dkey, dval = own_grad[h]
        for b in range(1, reach + 1):
            dkey = dkey + gr_in[b - 1, 0, :, cols[h]].astype(F32)
            dval = dval + gr_in[b - 1, 1, :, cols[h]].astype(F32)
        kg_ref[:, cols[h]] = dkey.astype(BF)
        vg_ref[:, cols[h]] = dval.astype(BF)

    for b in range(1, reach + 1):
        send_wait_if(up_ok(b), kv_copies(b))
        send_wait_if(down_ok(b), grad_copies(b))
    for r in range(rounds):
        send_wait_if(up_ok(1 << r), [fm_copy(r), fa_copy(r)])
        send_wait_if(down_ok(1 << r), [bk_copy(r)])
    for step in range(1, head_n):
        head_copy(step).wait_send()
    for step in range(1, seq_n):
        gain_copy(step).wait_send()


def body(att_query, att_key, att_value, norm_gain, dn_query, dn_key, write_rate, log_decay, out_grad):
    rows, heads, width = att_query.shape
    seq_n, head_n = lax.axis_size("seq"), lax.axis_size("head")
    reach = max(1, WIN // rows)
    rounds = max(1, (seq_n - 1).bit_length())
    wide = heads * width

    def flat(a):
        return a.reshape(rows, wide)

    big = jax.ShapeDtypeStruct((rows, wide), BF)
    thin = jax.ShapeDtypeStruct((rows, heads), F32)
    outs = [big, big, big, big, jax.ShapeDtypeStruct((heads, width), F32), big, big, thin, thin]
    dma = pltpu.SemaphoreType.DMA
    scratch = [
        pltpu.VMEM((reach, 2, rows, wide), BF),
        pltpu.VMEM((rounds, wide, width), BF),
        pltpu.VMEM((rounds, wide, width), BF),
        pltpu.VMEM((rounds, wide, width), BF),
        pltpu.VMEM((rounds, wide, width), BF),
        pltpu.VMEM((rounds, 2 * wide, width), BF),
        pltpu.VMEM((rounds, 2 * wide, width), BF),
        pltpu.VMEM((16, rows), F32),
        pltpu.VMEM((max(1, head_n - 1), 16, rows), F32),
        pltpu.VMEM((8, width), F32),
        pltpu.VMEM((max(1, seq_n - 1), 8, width), F32),
        pltpu.VMEM((reach, 2, rows, wide), BF),
        pltpu.VMEM((reach, 2, rows, wide), BF),
        pltpu.VMEM((heads, rows, rows), F32),
        pltpu.VMEM((heads, rows, rows), F32),
        pltpu.VMEM((heads, rows, rows), F32),
        pltpu.VMEM((heads, rows, rows), F32),
        pltpu.VMEM((heads, reach + 1, rows, rows), F32),
        pltpu.VMEM((heads, reach + 1, rows, rows), BF),
        dma((reach, 2)), dma((reach, 2)),
        dma((rounds,)), dma((rounds,)),
        dma((rounds,)), dma((rounds,)),
        dma((rounds,)), dma((rounds,)),
        dma((max(1, head_n - 1),)), dma((max(1, head_n - 1),)),
        dma((max(1, seq_n - 1),)), dma((max(1, seq_n - 1),)),
        dma((reach, 2)), dma((reach, 2)),
    ]
    vmem = pl.BlockSpec(memory_space=pltpu.VMEM)
    results = pl.pallas_call(
        functools.partial(kernel, seq_n, head_n, reach, rounds, heads, width),
        out_shape=outs,
        in_specs=[vmem] * 9,
        out_specs=[vmem] * 9,
        scratch_shapes=scratch,
        compiler_params=pltpu.CompilerParams(
            collective_id=0, has_side_effects=True, vmem_limit_bytes=48 * 1024 * 1024
        ),
    )(
        flat(att_query), flat(att_key), flat(att_value), norm_gain, flat(dn_query), flat(dn_key),
        write_rate, log_decay, flat(out_grad),
    )

    def tall(a):
        return a.reshape(rows, heads, width)

    o, qg, kg, vg, gg, dqg, dkg, rg, cg = results
    return (tall(o), tall(qg), tall(kg), tall(vg), gg, tall(dqg), tall(dkg), rg, cg)


def solution(mesh):
    cube = P("seq", "head", None)
    pair = P("seq", "head")
    return jax.shard_map(
        body,
        mesh=mesh,
        in_specs=(cube, cube, cube, P("head", None), cube, cube, pair, pair, cube),
        out_specs=(cube, cube, cube, cube, P("head", None), cube, cube, pair, pair),
        check_vma=False,
    )
```

time: 709 us -> 101 us (0.14); the launches traced: 695 us -> 100 us
  other arithmetic: 272 us -> 0 us
  matrix products: 159 us -> 0 us
  Pallas kernels: 0 us -> 89.5 us
  starting transfers between devices: 82.4 us -> 0 us
  waiting for transfers between devices: 76 us -> 0 us
  local copies, waits for them, and re-layouts: 67.5 us -> 10.3 us
  blocking collectives: 35 us -> 0 us
    another operation x100 -> x0, other arithmetic: 223 us -> none  [the longest x72 217 us: delta_block(): jax.scipy.linalg.solve_triangular(system, target, lower=True, unit_diagon...]
    dot_general x124 -> x0, matrix products: 139 us -> none  [the longest x16 22.6 us: delta_block(): jnp.einsum('nex,nxp->nep', query_vectors, memory_state, precision=MATMUL_...]
    pallas_call x0 -> x1, Pallas kernels: none -> 89.5 us  [body(): pl.pallas_call(functools.partial(kernel, seq_n, head_n, reach, rounds, he...]
    ppermute x30 -> x0, starting transfers between devices: 82.4 us -> none  [shifted_2(): return lax.ppermute(block, axis, route)]
    ppermute x30 -> x0, waiting for transfers between devices: 76 us -> none  [shifted_2(): return lax.ppermute(block, axis, route)]
    psum x3 -> x0, blocking collectives: 35 us -> none  [the longest x1 23.6 us: body(): gain_grad = lax.psum(gain_part, 'seq')]
    reduce_sum x23 -> x0, other arithmetic: 20.8 us -> none  [the longest x4 4.44 us: delta_block(): state_increment[:, :, None] * retrieved_values]
    another operation x20 -> x0, matrix products: 19.7 us -> none  [delta_block(): jax.scipy.linalg.solve_triangular(system, target, lower=True, unit_diagon...]
  transfers between devices with their start and end apart: 30 -> 0, of which waited for: 21 -> 0; matrix products, arithmetic and copies ran while one was open for 3% -> 0% of each run, Pallas kernels for 0% -> 0%
where the time goes in v1:
time: 101 us; the launch traced here: 100 us
  Pallas kernels  89.5 us (89%)
  local copies, waits for them, and re-layouts  10.3 us (10%)
    pallas_call x1, Pallas kernels, body(): pl.pallas_call(functools.partial(kernel, seq_n, head_n, reach, rounds, he...  89.5 us
    unnamed x23, local copies, waits for them, and re-layouts  6.02 us
    reshape x6, local copies, waits for them, and re-layouts, tall(): return a.reshape(rows, heads, width)  4.15 us

profile of v1, /device:TPU:10, one launch (start us, length us, event | category | flops | bytes accessed | tf_op | source)
XLA Modules:
  0.0 100.5 jit_solution(3472024581557658299)
XLA Ops:
  0.6 0.0 copy-start.7
  0.7 0.0 copy-start.8
  0.7 0.7 copy-done.7
  1.3 0.0 copy-start.1
  1.3 0.0 copy-start.2
  1.3 0.1 copy.18.rate_ref
  1.5 0.0 copy-done.8
  1.5 0.1 copy.19.decay_ref
  1.6 0.6 copy-done.1
  2.2 0.1 copy-done.2
  2.3 0.0 copy-start.3
  2.3 0.0 copy-start.4
  2.3 0.9 copy-done.3
  3.2 0.1 copy-done.4
  3.3 0.0 copy-start.5
  3.3 0.0 copy-start.6
  3.3 0.9 copy-done.5
  4.2 0.1 copy-done.6
  4.3 0.0 copy-start
  4.3 0.7 copy-done
  4.9 89.5 %shard_map.160 = (bf16[256,256]{1,0:T(8,128)(2,1)S(1)}, bf16[256,256]{1,0:T(8,128)(2,1)S(1)}, bf16[256,256]{1,0:T(8,128)(2,1)S(1)}, bf16[256,256]{1,0:T(8,128)(2...) custom-call(bf16[256,256]{1,0:T(8,128)(2,1)S(1)} %get-tuple-element., ...), custom_call_target="tpu_custom_call" | custom-call | tf_op jit(solution)/shard_map/pallas_call | solution.py:504
  94.4 0.7 reshape.60
  95.1 0.7 copy.20
  95.8 0.7 copy.21
  96.4 0.7 reshape.61
  97.1 0.7 reshape.62
  97.8 0.7 reshape.63
  98.5 0.7 reshape.64
  99.2 0.7 reshape.65
  99.9 0.6 copy.35
  (3 shorter events, 0.1 us)
Async XLA Ops:
  0.6 0.7 copy-start.7
  0.7 0.8 copy-start.8
  1.3 0.9 copy-start.1
  1.3 1.0 copy-start.2
  2.3 0.9 copy-start.3
  2.3 1.0 copy-start.4
  3.3 0.9 copy-start.5
  3.3 1.0 copy-start.6
  4.3 0.7 copy-start

commit v2 on v1

--- a/solution.py
+++ b/solution.py
@@ -52,7 +52,7 @@
     seq_n, head_n, reach, rounds, heads, width,
     q_ref, k_ref, v_ref, gain_ref, dq_ref, dk_ref, rate_ref, decay_ref, og_ref,
     out_ref, qg_ref, kg_ref, vg_ref, gg_ref, dqg_ref, dkg_ref, rg_ref, cg_ref,
-    kv_in, fm_out, fm_in, fa_out, fa_in, bk_out, bk_in, hs_out, hs_in, gn_out, gn_in, gr_out, gr_in,
+    kv_in, fm_out, fm_in, fa_out, fa_in, bk_out, bk_in, hs_out, hs_in, gn_out, gn_in, gr_out, gr_in, gx_in,
     t_s, ratio_s, p_s, kkr_s, score_s, weight_s,
     kv_ss, kv_rs, fm_ss, fm_rs, fa_ss, fa_rs, bk_ss, bk_rs, hs_ss, hs_rs, gn_ss, gn_rs, gr_ss, gr_rs,
 ):
@@ -81,6 +81,29 @@
             for i, ref in enumerate((k_ref, v_ref))
         ]
 
+    odd = lax.rem(me, 2) == 1
+    even = jnp.logical_not(odd)
+    partner = me + 1 - 2 * lax.rem(me, 2)
+
+    def partner_copy(src, dst, send_sem, recv_sem):
+        return pltpu.make_async_remote_copy(
+            src_ref=src, dst_ref=dst, send_sem=send_sem, recv_sem=recv_sem,
+            device_id={"seq": partner}, device_id_type=MESH,
+        )
+
+    def hand_copies(b, slot):
+        source = [k_ref, v_ref] if slot == 0 else [kv_in.at[slot - 1, i] for i in range(2)]
+        return [
+            partner_copy(source[i], kv_in.at[b - 1, i], kv_ss.at[b - 1, i], kv_rs.at[b - 1, i])
+            for i in range(2)
+        ]
+
+    def cross_copies(b):
+        return [
+            partner_copy(gr_out.at[b - 1, i], gx_in.at[b - 1, i], gr_ss.at[b - 1, i], gr_rs.at[b - 1, i])
+            for i in range(2)
+        ]
+
     def grad_copies(b):
         return [
             seq_copy(gr_out.at[b - 1, i], gr_in.at[b - 1, i], gr_ss.at[b - 1, i], gr_rs.at[b - 1, i], -b)
@@ -127,6 +150,10 @@
         @pl.when(jnp.logical_not(down_ok(b)))
         def _():
             kv_in[b - 1] = jnp.zeros(kv_in.shape[1:], BF)
+
+        @pl.when(partner - b < 0)
+        def _():
+            gx_in[b - 1] = jnp.zeros(gx_in.shape[1:], BF)
 
         @pl.when(jnp.logical_not(up_ok(b)))
         def _():
@@ -148,8 +175,15 @@
         pl.semaphore_signal(barrier, inc=1, device_id={"head": lax.rem(my_head + step, head_n)}, device_id_type=MESH)
     pl.semaphore_wait(barrier, seq_n + head_n - 2)
 
-    for b in range(1, reach + 1):
+    for b in range(2, reach + 1, 2):
         start_if(up_ok(b), kv_copies(b))
+    start_if(even, hand_copies(1, 0))
+
+    def hand_on(slot):
+        recv_if(down_ok(slot), kv_copies(slot))
+        if slot + 1 < reach:
+            start_if(jnp.logical_and(even, partner - (slot + 1) >= 0), hand_copies(slot + 1, slot))
+        start_if(jnp.logical_and(odd, partner - (slot - 1) >= 0), hand_copies(slot - 1, slot))
 
     at_row = lax.broadcasted_iota(jnp.int32, (rows, rows), 0)
     at_col = lax.broadcasted_iota(jnp.int32, (rows, rows), 1)
@@ -202,6 +236,10 @@
             y = dot3(x, jnp.where(off, state[h]["system"], 0.0))
             inverse_of[h] = x - dot3(y, x)
         level += 1
+        if level == 5:
+            hand_on(2)
+    for slot in range(4, reach + 1, 2):
+        hand_on(slot)
     for h in range(heads):
         s = state[h]
         t = inverse_of[h]
@@ -262,8 +300,8 @@
     scale = width ** (-0.5)
 
     def score_block(b):
-        if b > 0:
-            recv_if(down_ok(b), kv_copies(b))
+        if b % 2 == 1:
+            recv_if(down_ok(b), hand_copies(b, 0))
         for h in range(heads):
             keys = k_ref[:, cols[h]] if b == 0 else kv_in[b - 1, 0, :, cols[h]]
             sc = dot(q_ref[:, cols[h]], keys, NT) * scale
@@ -290,7 +328,7 @@
         dn = dot3(p_s[h], s["dout"], TN) + dot3(s["kr"], s["eb"])
         s["r"] = dot3(t_s[h], dn, TN)
         s["vg"] = (s["rate"] * s["r"]).astype(BF).astype(F32)
-    for b in range(1, reach + 1):
+    for b in list(range(2, reach + 1, 2)) + list(range(1, reach + 1, 2)):
         score_block(b)
     square = 0.0
     inner = 0.0
@@ -366,7 +404,8 @@
         s["mean"] = mean
         s["dqa"] = 0.0
     own_grad = []
-    for b in list(range(reach, 0, -1)) + [0]:
+    turn = 0
+    for b in list(range(reach - 1, 0, -2)) + list(range(reach, 0, -2)) + [0]:
         for h in range(heads):
             s = state[h]
             keys = k_ref[:, cols[h]] if b == 0 else kv_in[b - 1, 0, :, cols[h]]
@@ -381,21 +420,34 @@
                 gr_out[b - 1, 1, :, cols[h]] = dval.astype(BF)
             else:
                 own_grad.append((dkey, dval))
-        if b > 0:
-            start_if(down_ok(b), grad_copies(b))
-        if reach - b < rounds and b > 0:
-            r = reach - b
-            add_take(r)
-            if r < rounds - 1:
-                add_send(r + 1)
-    for r in range(reach, rounds):
+        if b % 2 == 1:
+            start_if(down_ok(b), cross_copies(b))
+        if turn < rounds:
+            add_take(turn)
+            if turn < rounds - 1:
+                add_send(turn + 1)
+        turn += 1
+    for r in range(turn, rounds):
         add_take(r)
         if r < rounds - 1:
             add_send(r + 1)
     for h in range(heads):
         qg_ref[:, cols[h]] = state[h]["dqa"].astype(BF)
 
-    for h in range(heads):
+    def cross_add(b):
+        recv_if(partner - b >= 0, cross_copies(b))
+        if b > 1:
+            @pl.when(jnp.logical_and(even, down_ok(b - 1)))
+            def _():
+                total = gr_out[b - 2].astype(F32) + gx_in[b - 1].astype(F32)
+                gr_out[b - 2] = total.astype(BF)
+
+        @pl.when(jnp.logical_and(odd, down_ok(b + 1)))
+        def _():
+            total = gr_out[b].astype(F32) + gx_in[b - 1].astype(F32)
+            gr_out[b] = total.astype(BF)
+
+    def finish(h):
         s = state[h]
         start, later = s["ea"], s["eb"]
         q, k, rate, gamma, retain = s["q"], s["k"], s["rate"], s["gamma"], s["retain"]
@@ -431,24 +483,35 @@
         dqg_ref[:, cols[h]] = (s["rq"] * (dq - q * row_sum(q * dq))).astype(BF)
         dkg_ref[:, cols[h]] = (s["rk"] * (dk - k * row_sum(k * dk))).astype(BF)
 
+    for b in range(reach - 1, 0, -2):
+        cross_add(b)
+        start_if(down_ok(b + 1), grad_copies(b + 1))
+    for h in range(heads):
+        finish(h)
+
     gain = gn_out[...]
     for step in range(1, seq_n):
         gain_copy(step).wait_recv()
         gain = gain + gn_in[step - 1]
     gg_ref[...] = gain[0:heads]
-    for b in range(reach, 0, -1):
+    for b in range(reach, 0, -2):
         recv_if(up_ok(b), grad_copies(b))
     for h in range(heads):
         dkey, dval = own_grad[h]
-        for b in range(1, reach + 1):
+        dkey = dkey + jnp.where(even, gx_in[0, 0, :, cols[h]].astype(F32), 0.0)
+        dval = dval + jnp.where(even, gx_in[0, 1, :, cols[h]].astype(F32), 0.0)
+        for b in range(2, reach + 1, 2):
             dkey = dkey + gr_in[b - 1, 0, :, cols[h]].astype(F32)
             dval = dval + gr_in[b - 1, 1, :, cols[h]].astype(F32)
         kg_ref[:, cols[h]] = dkey.astype(BF)
         vg_ref[:, cols[h]] = dval.astype(BF)
 
-    for b in range(1, reach + 1):
+    for b in range(2, reach + 1, 2):
         send_wait_if(up_ok(b), kv_copies(b))
         send_wait_if(down_ok(b), grad_copies(b))
+    for b in range(1, reach + 1, 2):
+        send_wait_if(partner - b >= 0, hand_copies(b, 0))
+        send_wait_if(down_ok(b), cross_copies(b))
     for r in range(rounds):
         send_wait_if(up_ok(1 << r), [fm_copy(r), fa_copy(r)])
         send_wait_if(down_ok(1 << r), [bk_copy(r)])
@@ -484,6 +547,7 @@
         pltpu.VMEM((max(1, head_n - 1), 16, rows), F32),
         pltpu.VMEM((8, width), F32),
         pltpu.VMEM((max(1, seq_n - 1), 8, width), F32),
+        pltpu.VMEM((reach, 2, rows, wide), BF),
         pltpu.VMEM((reach, 2, rows, wide), BF),
         pltpu.VMEM((reach, 2, rows, wide), BF),
         pltpu.VMEM((heads, rows, rows), F32),

time: 101 us -> 88.1 us (0.87)
  Pallas kernels: 89.5 us -> 76.9 us
    pallas_call x1, Pallas kernels: 89.5 us -> 76.9 us  [body(): pl.pallas_call(functools.partial(kernel, seq_n, head_n, reach, rounds, he...]
where the time goes in v2:
time: 88.1 us; the launch traced here: 87.9 us
  Pallas kernels  76.9 us (87%)
  local copies, waits for them, and re-layouts  10.3 us (12%)
    pallas_call x1, Pallas kernels, body(): pl.pallas_call(functools.partial(kernel, seq_n, head_n, reach, rounds, he...  76.9 us
    unnamed x23, local copies, waits for them, and re-layouts  6.02 us
    reshape x6, local copies, waits for them, and re-layouts, tall(): return a.reshape(rows, heads, width)  4.15 us

profile of v2, /device:TPU:10, one launch (start us, length us, event | category | flops | bytes accessed | tf_op | source)
XLA Modules:
  0.0 87.9 jit_solution(13627332895018305266)
XLA Ops:
  0.6 0.0 copy-start.7
  0.7 0.0 copy-start.8
  0.7 0.7 copy-done.7
  1.3 0.0 copy-start.1
  1.3 0.0 copy-start.2
  1.3 0.1 copy.18.rate_ref
  1.5 0.0 copy-done.8
  1.5 0.1 copy.19.decay_ref
  1.6 0.6 copy-done.1
  2.2 0.1 copy-done.2
  2.3 0.0 copy-start.3
  2.3 0.0 copy-start.4
  2.3 0.9 copy-done.3
  3.2 0.1 copy-done.4
  3.3 0.0 copy-start.5
  3.3 0.0 copy-start.6
  3.3 0.9 copy-done.5
  4.2 0.1 copy-done.6
  4.3 0.0 copy-start
  4.3 0.7 copy-done
  4.9 76.9 %shard_map.160 = (bf16[256,256]{1,0:T(8,128)(2,1)S(1)}, bf16[256,256]{1,0:T(8,128)(2,1)S(1)}, bf16[256,256]{1,0:T(8,128)(2,1)S(1)}, bf16[256,256]{1,0:T(8,128)(2...) custom-call(bf16[256,256]{1,0:T(8,128)(2,1)S(1)} %get-tuple-element., ...), custom_call_target="tpu_custom_call" | custom-call | tf_op jit(solution)/shard_map/pallas_call | solution.py:568
  81.9 0.7 reshape.60
  82.6 0.7 copy.20
  83.2 0.7 copy.21
  83.9 0.7 reshape.61
  84.6 0.7 reshape.62
  85.3 0.7 reshape.63
  86.0 0.7 reshape.64
  86.7 0.7 reshape.65
  87.4 0.6 copy.35
  (3 shorter events, 0.1 us)
Async XLA Ops:
  0.6 0.7 copy-start.7
  0.7 0.8 copy-start.8
  1.3 0.9 %copy-start.1 = (bf16[256,2,128]{2,1,0:T(2,128)(2,1)S(1)}, bf16[256,2,128]{2,1,0:T(2,128)(2,1)}, u32[]{:S(2)}) copy-start(bf16[256,2,128]{2,1,0:T(2,128)(2,1)} %param.10) | copy-start | bytes 393220
  1.3 1.0 %copy-start.2 = (bf16[256,2,128]{2,1,0:T(2,128)(2,1)S(1)}, bf16[256,2,128]{2,1,0:T(2,128)(2,1)}, u32[]{:S(2)}) copy-start(bf16[256,2,128]{2,1,0:T(2,128)(2,1)} %param.9) | copy-start | bytes 393220
  2.3 0.9 %copy-start.3 = (bf16[256,2,128]{2,1,0:T(2,128)(2,1)S(1)}, bf16[256,2,128]{2,1,0:T(2,128)(2,1)}, u32[]{:S(2)}) copy-start(bf16[256,2,128]{2,1,0:T(2,128)(2,1)} %param.13) | copy-start | bytes 393220
  2.3 1.0 %copy-start.4 = (bf16[256,2,128]{2,1,0:T(2,128)(2,1)S(1)}, bf16[256,2,128]{2,1,0:T(2,128)(2,1)}, u32[]{:S(2)}) copy-start(bf16[256,2,128]{2,1,0:T(2,128)(2,1)} %param.11) | copy-start | bytes 393220
  3.3 0.9 %copy-start.5 = (bf16[256,2,128]{2,1,0:T(2,128)(2,1)S(1)}, bf16[256,2,128]{2,1,0:T(2,128)(2,1)}, u32[]{:S(2)}) copy-start(bf16[256,2,128]{2,1,0:T(2,128)(2,1)} %param.17) | copy-start | bytes 393220
  3.3 1.0 %copy-start.6 = (bf16[256,2,128]{2,1,0:T(2,128)(2,1)S(1)}, bf16[256,2,128]{2,1,0:T(2,128)(2,1)}, u32[]{:S(2)}) copy-start(bf16[256,2,128]{2,1,0:T(2,128)(2,1)} %param.14) | copy-start | bytes 393220
  4.3 0.7 copy-start

commit v3 on v2

--- a/solution.py
+++ b/solution.py
@@ -106,7 +106,7 @@
 
     def grad_copies(b):
         return [
-            seq_copy(gr_out.at[b - 1, i], gr_in.at[b - 1, i], gr_ss.at[b - 1, i], gr_rs.at[b - 1, i], -b)
+            seq_copy(gr_out.at[b - 1, i], gr_in.at[b - 1, i], gr_ss.at[b - 1, i], gr_rs.at[b - 1, i], -2)
             for i in range(2)
         ]
 
@@ -155,7 +155,7 @@
         def _():
             gx_in[b - 1] = jnp.zeros(gx_in.shape[1:], BF)
 
-        @pl.when(jnp.logical_not(up_ok(b)))
+        @pl.when(jnp.logical_not(up_ok(2)))
         def _():
             gr_in[b - 1] = jnp.zeros(gr_in.shape[1:], BF)
     for r in range(rounds):
@@ -313,47 +313,55 @@
                 sc = jnp.where(down_ok(b), sc, -1e30)
             score_s[h, b] = sc
 
-    back_send(0)
-    forward_send(0)
-    score_block(0)
-    for r in range(rounds):
-        back_take(r)
-        if r < rounds - 1:
-            back_send(r + 1)
-        forward_take(r)
-        if r < rounds - 1:
-            forward_send(r + 1)
-    for h in range(heads):
+    def attend(h):
         s = state[h]
-        dn = dot3(p_s[h], s["dout"], TN) + dot3(s["kr"], s["eb"])
-        s["r"] = dot3(t_s[h], dn, TN)
-        s["vg"] = (s["rate"] * s["r"]).astype(BF).astype(F32)
-    for b in list(range(2, reach + 1, 2)) + list(range(1, reach + 1, 2)):
-        score_block(b)
-    square = 0.0
-    inner = 0.0
-    for h in range(heads):
-        s = state[h]
-        top = row_sum(jnp.zeros((rows, 128), F32)) - 1e30
-        for b in range(reach + 1):
+        top = jnp.max(score_s[h, 0], axis=1, keepdims=True)
+        for b in range(1, reach + 1):
             top = jnp.maximum(top, jnp.max(score_s[h, b], axis=1, keepdims=True))
         total = 0.0
         for b in range(reach + 1):
             e = jnp.exp(score_s[h, b] - top)
             score_s[h, b] = e
             total = total + row_sum(e)
+        share = 1.0 / total
         attended = 0.0
         for b in range(reach + 1):
-            w = score_s[h, b] / total
+            w = score_s[h, b] * share
             score_s[h, b] = w
             wb = w.astype(BF)
             weight_s[h, b] = wb
             values = v_ref[:, cols[h]] if b == 0 else kv_in[b - 1, 1, :, cols[h]]
             attended = attended + dot(wb, values)
         s["att"] = attended
+
+    back_send(0)
+    forward_send(0)
+    score_block(0)
+    beside = [[2], list(range(4, reach + 1, 2)) + list(range(1, reach + 1, 2))]
+    for r in range(max(rounds, 3)):
+        if r < rounds:
+            back_take(r)
+            if r < rounds - 1:
+                back_send(r + 1)
+            forward_take(r)
+            if r < rounds - 1:
+                forward_send(r + 1)
+        if r < 2:
+            for b in beside[r]:
+                score_block(b)
+        if r == 1:
+            for h in range(heads):
+                attend(h)
+    square = 0.0
+    inner = 0.0
+    for h in range(heads):
+        s = state[h]
+        dn = dot3(p_s[h], s["dout"], TN) + dot3(s["kr"], s["eb"])
+        s["r"] = dot3(t_s[h], dn, TN)
+        s["vg"] = (s["rate"] * s["r"]).astype(BF).astype(F32)
         s["weighted"] = s["vg"] * gain_ref[h : h + 1, :]
-        square = square + row_sum(attended * attended)
-        inner = inner + row_sum(s["weighted"] * attended)
+        square = square + row_sum(s["att"] * s["att"])
+        inner = inner + row_sum(s["weighted"] * s["att"])
     hs_out[0:8] = jnp.broadcast_to(to_row(square), (8, rows))
     hs_out[8:16] = jnp.broadcast_to(to_row(inner), (8, rows))
     for step in range(1, head_n):
@@ -396,12 +404,7 @@
 
     for h in range(heads):
         s = state[h]
-        mean = 0.0
-        for b in range(reach + 1):
-            values = v_ref[:, cols[h]] if b == 0 else kv_in[b - 1, 1, :, cols[h]]
-            dw = dot(s["datt"], values, NT).astype(BF).astype(F32)
-            mean = mean + row_sum(dw * score_s[h, b])
-        s["mean"] = mean
+        s["mean"] = row_sum(s["datt"].astype(F32) * s["att"])
         s["dqa"] = 0.0
     own_grad = []
     turn = 0
@@ -483,10 +486,25 @@
         dqg_ref[:, cols[h]] = (s["rq"] * (dq - q * row_sum(q * dq))).astype(BF)
         dkg_ref[:, cols[h]] = (s["rk"] * (dk - k * row_sum(k * dk))).astype(BF)
 
+    def chain_add(b):
+        ready = jnp.logical_and(up_ok(2), me + 2 - b >= 0)
+        recv_if(ready, grad_copies(b))
+
+        @pl.when(jnp.logical_and(ready, down_ok(b - 2)))
+        def _():
+            total = gr_out[b - 3].astype(F32) + gr_in[b - 1].astype(F32)
+            gr_out[b - 3] = total.astype(BF)
+
+    finished = 0
     for b in range(reach - 1, 0, -2):
         cross_add(b)
+        if b + 3 <= reach:
+            chain_add(b + 3)
         start_if(down_ok(b + 1), grad_copies(b + 1))
-    for h in range(heads):
+        if finished < heads:
+            finish(finished)
+            finished += 1
+    for h in range(finished, heads):
         finish(h)
 
     gain = gn_out[...]
@@ -494,15 +512,13 @@
         gain_copy(step).wait_recv()
         gain = gain + gn_in[step - 1]
     gg_ref[...] = gain[0:heads]
-    for b in range(reach, 0, -2):
-        recv_if(up_ok(b), grad_copies(b))
+    recv_if(up_ok(2), grad_copies(2))
     for h in range(heads):
         dkey, dval = own_grad[h]
         dkey = dkey + jnp.where(even, gx_in[0, 0, :, cols[h]].astype(F32), 0.0)
         dval = dval + jnp.where(even, gx_in[0, 1, :, cols[h]].astype(F32), 0.0)
-        for b in range(2, reach + 1, 2):
-            dkey = dkey + gr_in[b - 1, 0, :, cols[h]].astype(F32)
-            dval = dval + gr_in[b - 1, 1, :, cols[h]].astype(F32)
+        dkey = dkey + gr_in[1, 0, :, cols[h]].astype(F32)
+        dval = dval + gr_in[1, 1, :, cols[h]].astype(F32)
         kg_ref[:, cols[h]] = dkey.astype(BF)
         vg_ref[:, cols[h]] = dval.astype(BF)
 

time: 88.1 us -> 85.2 us (0.967)
  Pallas kernels: 76.9 us -> 74 us
    pallas_call x1, Pallas kernels: 76.9 us -> 74 us  [body(): pl.pallas_call(functools.partial(kernel, seq_n, head_n, reach, rounds, he...]
where the time goes in v3:
time: 85.2 us; the launch traced here: 85 us
  Pallas kernels  74 us (87%)
  local copies, waits for them, and re-layouts  10.3 us (12%)
    pallas_call x1, Pallas kernels, body(): pl.pallas_call(functools.partial(kernel, seq_n, head_n, reach, rounds, he...  74 us
    unnamed x23, local copies, waits for them, and re-layouts  6.02 us
    reshape x6, local copies, waits for them, and re-layouts, tall(): return a.reshape(rows, heads, width)  4.15 us

profile of v3, /device:TPU:10, one launch (start us, length us, event | category | flops | bytes accessed | tf_op | source)
XLA Modules:
  0.0 85.0 jit_solution(16909698120287486655)
XLA Ops:
  0.6 0.0 copy-start.7
  0.7 0.0 copy-start.8
  0.7 0.7 copy-done.7
  1.3 0.0 copy-start.1
  1.3 0.0 copy-start.2
  1.3 0.1 copy.18.rate_ref
  1.5 0.0 copy-done.8
  1.5 0.1 copy.19.decay_ref
  1.6 0.6 copy-done.1
  2.2 0.1 copy-done.2
  2.3 0.0 copy-start.3
  2.3 0.0 copy-start.4
  2.3 0.9 %copy-done.3 = bf16[256,2,128]{2,1,0:T(2,128)(2,1)S(1)} copy-done((bf16[256,2,128]{2,1,0:T(2,128)(2,1)S(1)}, bf16[256,2,128]{2,1,0:T(2,128)(2,1)}, u32[]{:S(2)}) %copy-start.3) | copy-done | bytes 131096
  3.2 0.1 copy-done.4
  3.3 0.0 copy-start.5
  3.3 0.0 copy-start.6
  3.3 0.9 %copy-done.5 = bf16[256,2,128]{2,1,0:T(2,128)(2,1)S(1)} copy-done((bf16[256,2,128]{2,1,0:T(2,128)(2,1)S(1)}, bf16[256,2,128]{2,1,0:T(2,128)(2,1)}, u32[]{:S(2)}) %copy-start.5) | copy-done | bytes 131096
  4.2 0.1 copy-done.6
  4.3 0.0 copy-start
  4.3 0.7 copy-done
  4.9 74.0 %shard_map.160 = (bf16[256,256]{1,0:T(8,128)(2,1)S(1)}, bf16[256,256]{1,0:T(8,128)(2,1)S(1)}, bf16[256,256]{1,0:T(8,128)(2,1)S(1)}, bf16[256,256]{1,0:T(8,128)(2...) custom-call(bf16[256,256]{1,0:T(8,128)(2,1)S(1)} %get-tuple-element., ...), custom_call_target="tpu_custom_call" | custom-call | tf_op jit(solution)/shard_map/pallas_call | solution.py:584
  79.0 0.7 reshape.60
  79.7 0.7 copy.20
  80.3 0.7 copy.21
  81.0 0.7 reshape.61
  81.7 0.7 reshape.62
  82.3 0.7 reshape.63
  83.0 0.7 reshape.64
  83.7 0.7 reshape.65
  84.4 0.6 copy.35
  (3 shorter events, 0.1 us)
Async XLA Ops:
  0.6 0.7 copy-start.7
  0.7 0.8 copy-start.8
  1.3 0.9 %copy-start.1 = (bf16[256,2,128]{2,1,0:T(2,128)(2,1)S(1)}, bf16[256,2,128]{2,1,0:T(2,128)(2,1)}, u32[]{:S(2)}) copy-start(bf16[256,2,128]{2,1,0:T(2,128)(2,1)} %param.10) | copy-start | bytes 393220
  1.3 1.0 %copy-start.2 = (bf16[256,2,128]{2,1,0:T(2,128)(2,1)S(1)}, bf16[256,2,128]{2,1,0:T(2,128)(2,1)}, u32[]{:S(2)}) copy-start(bf16[256,2,128]{2,1,0:T(2,128)(2,1)} %param.9) | copy-start | bytes 393220
  2.3 0.9 %copy-start.3 = (bf16[256,2,128]{2,1,0:T(2,128)(2,1)S(1)}, bf16[256,2,128]{2,1,0:T(2,128)(2,1)}, u32[]{:S(2)}) copy-start(bf16[256,2,128]{2,1,0:T(2,128)(2,1)} %param.13) | copy-start | bytes 393220
  2.3 1.0 %copy-start.4 = (bf16[256,2,128]{2,1,0:T(2,128)(2,1)S(1)}, bf16[256,2,128]{2,1,0:T(2,128)(2,1)}, u32[]{:S(2)}) copy-start(bf16[256,2,128]{2,1,0:T(2,128)(2,1)} %param.11) | copy-start | bytes 393220
  3.3 0.9 %copy-start.5 = (bf16[256,2,128]{2,1,0:T(2,128)(2,1)S(1)}, bf16[256,2,128]{2,1,0:T(2,128)(2,1)}, u32[]{:S(2)}) copy-start(bf16[256,2,128]{2,1,0:T(2,128)(2,1)} %param.17) | copy-start | bytes 393220
  3.3 1.0 %copy-start.6 = (bf16[256,2,128]{2,1,0:T(2,128)(2,1)S(1)}, bf16[256,2,128]{2,1,0:T(2,128)(2,1)}, u32[]{:S(2)}) copy-start(bf16[256,2,128]{2,1,0:T(2,128)(2,1)} %param.14) | copy-start | bytes 393220
  4.3 0.7 copy-start

commit v4 on v3

--- a/solution.py
+++ b/solution.py
@@ -228,13 +228,17 @@
     for h in range(heads):
         off = ((at_row >> 1) == (at_col >> 1))
         inverse_of.append(eye - jnp.where(off, state[h]["system"], 0.0))
+    system_halves = [halves(state[h]["system"]) for h in range(heads)]
     level = 1
     while (1 << level) < rows:
         off = ((at_row >> (level + 1)) == (at_col >> (level + 1))) & ((at_row >> level) != (at_col >> level))
+        keep = jnp.where(off, 1.0, 0.0).astype(BF)
         for h in range(heads):
             x = inverse_of[h]
-            y = dot3(x, jnp.where(off, state[h]["system"], 0.0))
-            inverse_of[h] = x - dot3(y, x)
+            xh, xl = halves(x)
+            sh, sl = (half * keep for half in system_halves[h])
+            yh, yl = halves(dot(xh, sh) + (dot(xh, sl) + dot(xl, sh)))
+            inverse_of[h] = x - (dot(yh, xh) + (dot(yh, xl) + dot(yl, xh)))
         level += 1
         if level == 5:
             hand_on(2)

time: 85.2 us -> 85.2 us (level)
  no operation moved by 1% of the time
where the time goes in v4:
time: 85.2 us; the launch traced here: 85 us
  Pallas kernels  74 us (87%)
  local copies, waits for them, and re-layouts  10.3 us (12%)
    pallas_call x1, Pallas kernels, body(): pl.pallas_call(functools.partial(kernel, seq_n, head_n, reach, rounds, he...  74 us
    unnamed x23, local copies, waits for them, and re-layouts  6.02 us
    reshape x6, local copies, waits for them, and re-layouts, tall(): return a.reshape(rows, heads, width)  4.15 us

profile of v4, /device:TPU:10, one launch (start us, length us, event | category | flops | bytes accessed | tf_op | source)
XLA Modules:
  0.0 85.0 jit_solution(8381943980603641693)
XLA Ops:
  0.6 0.0 copy-start.7
  0.7 0.0 copy-start.8
  0.7 0.7 copy-done.7
  1.3 0.0 copy-start.1
  1.3 0.0 copy-start.2
  1.3 0.1 copy.18.rate_ref
  1.5 0.0 copy-done.8
  1.5 0.1 copy.19.decay_ref
  1.6 0.6 copy-done.1
  2.2 0.1 copy-done.2
  2.3 0.0 copy-start.3
  2.3 0.0 copy-start.4
  2.3 0.9 %copy-done.3 = bf16[256,2,128]{2,1,0:T(2,128)(2,1)S(1)} copy-done((bf16[256,2,128]{2,1,0:T(2,128)(2,1)S(1)}, bf16[256,2,128]{2,1,0:T(2,128)(2,1)}, u32[]{:S(2)}) %copy-start.3) | copy-done | bytes 131096
  3.2 0.1 copy-done.4
  3.3 0.0 copy-start.5
  3.3 0.0 copy-start.6
  3.3 0.9 %copy-done.5 = bf16[256,2,128]{2,1,0:T(2,128)(2,1)S(1)} copy-done((bf16[256,2,128]{2,1,0:T(2,128)(2,1)S(1)}, bf16[256,2,128]{2,1,0:T(2,128)(2,1)}, u32[]{:S(2)}) %copy-start.5) | copy-done | bytes 131096
  4.2 0.1 copy-done.6
  4.3 0.0 copy-start
  4.3 0.7 copy-done
  4.9 74.0 %shard_map.160 = (bf16[256,256]{1,0:T(8,128)(2,1)S(1)}, bf16[256,256]{1,0:T(8,128)(2,1)S(1)}, bf16[256,256]{1,0:T(8,128)(2,1)S(1)}, bf16[256,256]{1,0:T(8,128)(2...) custom-call(bf16[256,256]{1,0:T(8,128)(2,1)S(1)} %get-tuple-element., ...), custom_call_target="tpu_custom_call" | custom-call | tf_op jit(solution)/shard_map/pallas_call | solution.py:588
  79.0 0.7 reshape.60
  79.7 0.7 copy.20
  80.3 0.7 copy.21
  81.0 0.7 reshape.61
  81.7 0.7 reshape.62
  82.4 0.7 reshape.63
  83.0 0.7 reshape.64
  83.7 0.7 reshape.65
  84.4 0.6 copy.35
  (3 shorter events, 0.1 us)
Async XLA Ops:
  0.6 0.7 copy-start.7
  0.7 0.8 copy-start.8
  1.3 0.9 %copy-start.1 = (bf16[256,2,128]{2,1,0:T(2,128)(2,1)S(1)}, bf16[256,2,128]{2,1,0:T(2,128)(2,1)}, u32[]{:S(2)}) copy-start(bf16[256,2,128]{2,1,0:T(2,128)(2,1)} %param.10) | copy-start | bytes 393220
  1.3 1.0 %copy-start.2 = (bf16[256,2,128]{2,1,0:T(2,128)(2,1)S(1)}, bf16[256,2,128]{2,1,0:T(2,128)(2,1)}, u32[]{:S(2)}) copy-start(bf16[256,2,128]{2,1,0:T(2,128)(2,1)} %param.9) | copy-start | bytes 393220
  2.3 0.9 %copy-start.3 = (bf16[256,2,128]{2,1,0:T(2,128)(2,1)S(1)}, bf16[256,2,128]{2,1,0:T(2,128)(2,1)}, u32[]{:S(2)}) copy-start(bf16[256,2,128]{2,1,0:T(2,128)(2,1)} %param.13) | copy-start | bytes 393220
  2.3 1.0 %copy-start.4 = (bf16[256,2,128]{2,1,0:T(2,128)(2,1)S(1)}, bf16[256,2,128]{2,1,0:T(2,128)(2,1)}, u32[]{:S(2)}) copy-start(bf16[256,2,128]{2,1,0:T(2,128)(2,1)} %param.11) | copy-start | bytes 393220
  3.3 0.9 %copy-start.5 = (bf16[256,2,128]{2,1,0:T(2,128)(2,1)S(1)}, bf16[256,2,128]{2,1,0:T(2,128)(2,1)}, u32[]{:S(2)}) copy-start(bf16[256,2,128]{2,1,0:T(2,128)(2,1)} %param.17) | copy-start | bytes 393220
  3.3 1.0 %copy-start.6 = (bf16[256,2,128]{2,1,0:T(2,128)(2,1)S(1)}, bf16[256,2,128]{2,1,0:T(2,128)(2,1)}, u32[]{:S(2)}) copy-start(bf16[256,2,128]{2,1,0:T(2,128)(2,1)} %param.14) | copy-start | bytes 393220
  4.3 0.7 copy-start
